TPU v7x, 32 devices: a whole 2x2x4 slice. The times are simulated.
32 devices in a mesh: dp: 8 (over z, x), mp: 4 (over y, core).
Axes of the slice: x: 2, y: 2, z: 4, core: 2. Of those that a mesh axis runs over, the one named last changes fastest.
Arguments:
- hidden_in: bfloat16 [12288, 768], P('dp'), may hold values from -6 to 6
- page_ids: int32 [12288], P('dp'), may hold values from 0 to 7, as said below
- pad_mask: int32 [12288], P('dp'), may hold values from 0 to 1, as said below
- boxes: int32 [12288, 2], P('dp'), may hold values from 0 to 999
- out_grad: bfloat16 [12288, 768], P('dp'), may hold values from -6 to 6
- attn_in: float32 [5, 768, 768], P(None, 'dp', 'mp'), may hold values from -0.21875 to 0.21875
- attn_in_moment: float32 [5, 768, 768], P(None, 'dp', 'mp'), may hold values from -20 to 20
- attn_in_second: float32 [5, 768, 768], P(None, 'dp', 'mp'), may hold values from 0.24576 to 2.4576
- attn_out: float32 [768, 768], P('mp', 'dp'), may hold values from -0.875 to 0.875
- attn_out_moment: float32 [768, 768], P('mp', 'dp'), may hold values from -10 to 10
- attn_out_second: float32 [768, 768], P('mp', 'dp'), may hold values from 0.12288 to 0.98304
- ffn_in: float32 [768, 3072], P('dp', 'mp'), may hold values from -0.21875 to 0.21875
- ffn_in_moment: float32 [768, 3072], P('dp', 'mp'), may hold values from -20 to 20
- ffn_in_second: float32 [768, 3072], P('dp', 'mp'), may hold values from 0.6144 to 4.9152
- ffn_out: float32 [3072, 768], P('mp', 'dp'), may hold values from -0.109375 to 0.109375
- ffn_out_moment: float32 [3072, 768], P('mp', 'dp'), may hold values from -32 to 32
- ffn_out_second: float32 [3072, 768], P('mp', 'dp'), may hold values from 1.2288 to 7.3728
- norm_weight: float32 [4, 768], P(None, 'dp'), may hold values from -0.9 to 1.5
- norm_moment: float32 [4, 768], P(None, 'dp'), may hold values from -64 to 64
- norm_second: float32 [4, 768], P(None, 'dp'), may hold values from 6.144 to 49.152
Outputs:
- mixed: bfloat16 [12288, 768], P('dp')
- input_grad: float32 [12288, 768], P('dp')
- new_attn_in: float32 [5, 768, 768], P(None, 'dp', 'mp')
- new_attn_in_moment: float32 [5, 768, 768], P(None, 'dp', 'mp')
- new_attn_in_second: float32 [5, 768, 768], P(None, 'dp', 'mp')
- new_attn_out: float32 [768, 768], P('mp', 'dp')
- new_attn_out_moment: float32 [768, 768], P('mp', 'dp')
- new_attn_out_second: float32 [768, 768], P('mp', 'dp')
- new_ffn_in: float32 [768, 3072], P('dp', 'mp')
- new_ffn_in_moment: float32 [768, 3072], P('dp', 'mp')
- new_ffn_in_second: float32 [768, 3072], P('dp', 'mp')
- new_ffn_out: float32 [3072, 768], P('mp', 'dp')
- new_ffn_out_moment: float32 [3072, 768], P('mp', 'dp')
- new_ffn_out_second: float32 [3072, 768], P('mp', 'dp')
- new_norm_weight: float32 [4, 768], P(None, 'dp')
- new_norm_moment: float32 [4, 768], P(None, 'dp')
- new_norm_second: float32 [4, 768], P(None, 'dp')
Inputs may be any that keep to these rules, and one draw needn't show every extreme that they name: `page_ids`: within each row of 512 tokens the page numbers start at 0, never fall, and each of the 8 pages holds at least one token. `pad_mask`: each row of 512 tokens ends with 1 to 64 padding tokens; all other tokens are 0.
All inputs are finite; a program needn't handle non-finite values.
Results may differ from a plain program's by a relative error of at most 0.02.
The roundings to bfloat16 on the way count: a program that leaves them out, or rounds other values in their place, can miss the bound.
Values may be sent and summed in bfloat16 or wider, within the bound.
A program may use at most 128 MiB of HBM per device.

v0:
```python
from functools import partial
import math

import jax
import jax.numpy as jnp
from jax import lax
from jax.sharding import PartitionSpec as P

D = 768
HEAD_DIM = 64
SEQ = 512
STEP = 10


epsilon_norm = 1e-12
epsilon_adam = 1e-08
beta_first = 0.9
beta_second = 0.999
rate_matrix = 0.05
rate_norm = 0.2
decay_matrix = 0.01
masked_score = -1e30


def box_embed(boxes):
    quarter = D // 4
    ladder = jnp.arange(quarter).astype(jnp.float32)
    frequency = jnp.exp(ladder * (-math.log(10000.0) / quarter))
    coords = boxes.astype(jnp.float32)
    across = coords[:, 0:1] * frequency[None, :]
    upward = coords[:, 1:2] * frequency[None, :]
    return jnp.concatenate(
        [jnp.sin(across), jnp.cos(across), jnp.sin(upward), jnp.cos(upward)], axis=1
    )


def layer_norm(values, scaling, offset):
    center = jnp.mean(values, axis=-1, keepdims=True)
    shifted = values - center
    spread = jnp.mean(shifted * shifted, axis=-1, keepdims=True)
    return shifted * lax.rsqrt(spread + epsilon_norm) * scaling + offset


def mask_of(page_numbers, padding):
    places = jnp.arange(page_numbers.shape[0])
    same_page = page_numbers[:, None] == page_numbers[None, :]
    usable = (padding[None, :] == 0) | (places[:, None] == places[None, :])
    return same_page & usable


def adam_step(weight, gradient, moment, second, rate, decay):
    moment_new = beta_first * moment + (1.0 - beta_first) * gradient
    second_new = beta_second * second + (1.0 - beta_second) * gradient * gradient
    moment_hat = moment_new / (1.0 - beta_first**STEP)
    second_hat = second_new / (1.0 - beta_second**STEP)
    weight_new = weight - rate * (
        moment_hat / (jnp.sqrt(second_hat) + epsilon_adam) + decay * weight
    )
    return (weight_new, moment_new, second_new)


def pair_scores(query_rows, key_rows, box_query, box_key, page_numbers, padding):
    left_side = jnp.concatenate([query_rows, query_rows, box_query], axis=-1)
    right_side = jnp.concatenate([key_rows, box_key, key_rows], axis=-1)
    scores = jnp.einsum(
        "qhe,khe->hqk", left_side, right_side, preferred_element_type=jnp.float32
    ) * HEAD_DIM ** (-0.5)
    allowed = mask_of(page_numbers, padding)
    return (jnp.where(allowed[None], scores, masked_score), left_side, right_side)


def forward_block(pieces):
    query_rows, key_rows, value_rows, box_query, box_key, page_numbers, padding = pieces
    scores, left_side, right_side = pair_scores(
        query_rows, key_rows, box_query, box_key, page_numbers, padding
    )
    highest_score = jnp.max(scores, axis=-1, keepdims=True)
    raised = jnp.exp(scores - highest_score)
    row_total = jnp.sum(raised, axis=-1, keepdims=True)
    softmax_out = (raised / row_total).astype(jnp.bfloat16)
    context = jnp.einsum(
        "hqk,khe->qhe", softmax_out, value_rows, preferred_element_type=jnp.float32
    )
    return (context.astype(jnp.bfloat16), highest_score, row_total)


def backward_block(pieces):
    (
        query_rows,
        key_rows,
        value_rows,
        box_query,
        box_key,
        page_numbers,
        padding,
        highest_score,
        row_total,
        grad_context,
    ) = pieces
    scores, left_side, right_side = pair_scores(
        query_rows, key_rows, box_query, box_key, page_numbers, padding
    )
    softmax_full = jnp.exp(scores - highest_score) / row_total
    grad_soft = jnp.einsum(
        "qhe,khe->hqk", grad_context, value_rows, preferred_element_type=jnp.float32
    )
    weighted = jnp.sum(softmax_full * grad_soft, axis=-1, keepdims=True)
    grad_scores = (softmax_full * (grad_soft - weighted)).astype(jnp.bfloat16)
    score_scale = HEAD_DIM ** (-0.5)
    grad_left = (
        jnp.einsum("hqk,khe->qhe", grad_scores, right_side, preferred_element_type=jnp.float32)
        * score_scale
    )
    grad_right = (
        jnp.einsum("hqk,qhe->khe", grad_scores, left_side, preferred_element_type=jnp.float32)
        * score_scale
    )
    grad_value = jnp.einsum(
        "hqk,qhe->khe",
        softmax_full.astype(jnp.bfloat16),
        grad_context,
        preferred_element_type=jnp.float32,
    )
    head_width = HEAD_DIM
    grad_query = grad_left[..., :head_width] + grad_left[..., head_width : 2 * head_width]
    grad_box_query = grad_left[..., 2 * head_width :]
    grad_key = grad_right[..., :head_width] + grad_right[..., 2 * head_width :]
    grad_box_key = grad_right[..., head_width : 2 * head_width]
    return (
        grad_query.astype(jnp.bfloat16),
        grad_key.astype(jnp.bfloat16),
        grad_value.astype(jnp.bfloat16),
        grad_box_query.astype(jnp.bfloat16),
        grad_box_key.astype(jnp.bfloat16),
    )


def per_device(
    hidden_in,
    page_ids,
    pad_mask,
    boxes,
    out_grad,
    attn_in,
    attn_in_moment,
    attn_in_second,
    attn_out,
    attn_out_moment,
    attn_out_second,
    ffn_in,
    ffn_in_moment,
    ffn_in_second,
    ffn_out,
    ffn_out_moment,
    ffn_out_second,
    norm_weight,
    norm_moment,
    norm_second,
):
    weight_in, weight_out, weight_up, weight_down = (
        lax.all_gather(attn_in.astype(jnp.bfloat16), "dp", axis=1, tiled=True),
        lax.all_gather(attn_out.astype(jnp.bfloat16), "dp", axis=1, tiled=True),
        lax.all_gather(ffn_in.astype(jnp.bfloat16), "dp", axis=0, tiled=True),
        lax.all_gather(ffn_out.astype(jnp.bfloat16), "dp", axis=1, tiled=True),
    )
    norm_full = lax.all_gather(norm_weight, "dp", axis=1, tiled=True)
    token_count = hidden_in.shape[0]
    block_count = token_count // SEQ
    group_width = weight_in.shape[2]
    heads_here = group_width // HEAD_DIM
    embed = box_embed(boxes).astype(jnp.bfloat16)
    text_proj = jnp.einsum(
        "td,sdc->stc", hidden_in, weight_in[:3], preferred_element_type=jnp.float32
    ).astype(jnp.bfloat16)
    box_proj = jnp.einsum(
        "td,sdc->stc", embed, weight_in[3:], preferred_element_type=jnp.float32
    ).astype(jnp.bfloat16)

    def per_block(values):
        return values.reshape(block_count, SEQ, heads_here, HEAD_DIM)

    blocked = (
        per_block(text_proj[0]),
        per_block(text_proj[1]),
        per_block(text_proj[2]),
        per_block(box_proj[0]),
        per_block(box_proj[1]),
        page_ids.reshape(block_count, SEQ),
        pad_mask.reshape(block_count, SEQ),
    )
    contexts, highest_score, row_total = lax.map(forward_block, blocked)
    context = contexts.reshape(token_count, group_width)
    attn_total = lax.psum(
        jnp.dot(context, weight_out, preferred_element_type=jnp.float32).astype(jnp.bfloat16), "mp"
    ).astype(jnp.float32)
    residual_one = hidden_in.astype(jnp.float32) + attn_total
    normed_one, norm_back_one = jax.vjp(layer_norm, residual_one, norm_full[0], norm_full[1])
    shared = normed_one.astype(jnp.bfloat16)
    pre_active = jnp.dot(shared, weight_up, preferred_element_type=jnp.float32)
    active_full, gelu_back = jax.vjp(partial(jax.nn.gelu, approximate=False), pre_active)
    active = active_full.astype(jnp.bfloat16)
    ffn_total = lax.psum(
        jnp.dot(active, weight_down, preferred_element_type=jnp.float32).astype(jnp.bfloat16), "mp"
    ).astype(jnp.float32)
    final, norm_back_two = jax.vjp(layer_norm, normed_one + ffn_total, norm_full[2], norm_full[3])
    mixed = final.astype(jnp.bfloat16)
    grad_two, scale_two, offset_two = norm_back_two(out_grad.astype(jnp.float32))
    grad_two_low = grad_two.astype(jnp.bfloat16)
    grad_down = jnp.einsum("tf,td->fd", active, grad_two_low, preferred_element_type=jnp.float32)
    grad_active = jnp.einsum(
        "td,fd->tf", grad_two_low, weight_down, preferred_element_type=jnp.float32
    )
    grad_pre = gelu_back(grad_active)[0].astype(jnp.bfloat16)
    grad_up = jnp.einsum("td,tf->df", shared, grad_pre, preferred_element_type=jnp.float32)
    ffn_back_term = jnp.einsum("tf,df->td", grad_pre, weight_up, preferred_element_type=jnp.float32)
    grad_normed = grad_two + lax.psum(ffn_back_term.astype(jnp.bfloat16), "mp").astype(jnp.float32)
    grad_one, scale_one, offset_one = norm_back_one(grad_normed)
    grad_one_low = grad_one.astype(jnp.bfloat16)
    grad_out = jnp.einsum("tc,td->cd", context, grad_one_low, preferred_element_type=jnp.float32)
    grad_context = jnp.einsum(
        "td,cd->tc", grad_one_low, weight_out, preferred_element_type=jnp.float32
    ).astype(jnp.bfloat16)
    backward_input = blocked + (highest_score, row_total, per_block(grad_context))
    block_grads = lax.map(backward_block, backward_input)
    flattened = [member.reshape(token_count, group_width) for member in block_grads]
    text_grads = jnp.stack(flattened[:3])
    box_grads = jnp.stack(flattened[3:])
    grad_in = jnp.concatenate(
        [
            jnp.einsum("td,stc->sdc", hidden_in, text_grads, preferred_element_type=jnp.float32),
            jnp.einsum("td,stc->sdc", embed, box_grads, preferred_element_type=jnp.float32),
        ],
        axis=0,
    )
    attn_back_term = jnp.einsum(
        "stc,sdc->td", text_grads, weight_in[:3], preferred_element_type=jnp.float32
    )
    input_grad = grad_one + lax.psum(attn_back_term.astype(jnp.bfloat16), "mp").astype(jnp.float32)
    grad_norm = jnp.stack([scale_one, offset_one, scale_two, offset_two])
    split_dims = (1, 1, 0, 1, 1)
    share_sizes = (
        attn_in.shape[1],
        attn_out.shape[1],
        ffn_in.shape[0],
        ffn_out.shape[1],
        norm_weight.shape[1],
    )
    summed = lax.psum((grad_in, grad_out, grad_up, grad_down, grad_norm), "dp")
    position = lax.axis_index("dp")
    reduced = tuple(
        (
            lax.dynamic_slice_in_dim(whole_sum, position * share_size, share_size, axis_dim)
            for whole_sum, share_size, axis_dim in zip(summed, share_sizes, split_dims)
        )
    )
    new_in = adam_step(
        attn_in, reduced[0], attn_in_moment, attn_in_second, rate_matrix, decay_matrix
    )
    new_out = adam_step(
        attn_out, reduced[1], attn_out_moment, attn_out_second, rate_matrix, decay_matrix
    )
    new_up = adam_step(ffn_in, reduced[2], ffn_in_moment, ffn_in_second, rate_matrix, decay_matrix)
    new_down = adam_step(
        ffn_out, reduced[3], ffn_out_moment, ffn_out_second, rate_matrix, decay_matrix
    )
    new_norm = adam_step(norm_weight, reduced[4], norm_moment, norm_second, rate_norm, 0.0)
    return (mixed, input_grad) + new_in + new_out + new_up + new_down + new_norm


def solution(mesh):
    return jax.shard_map(
        per_device,
        mesh=mesh,
        in_specs=(
            P("dp", None),
            P("dp"),
            P("dp"),
            P("dp", None),
            P("dp", None),
            P(None, "dp", "mp"),
            P(None, "dp", "mp"),
            P(None, "dp", "mp"),
            P("mp", "dp"),
            P("mp", "dp"),
            P("mp", "dp"),
            P("dp", "mp"),
            P("dp", "mp"),
            P("dp", "mp"),
            P("mp", "dp"),
            P("mp", "dp"),
            P("mp", "dp"),
            P(None, "dp"),
            P(None, "dp"),
            P(None, "dp"),
        ),
        out_specs=(
            P("dp", None),
            P("dp", None),
            P(None, "dp", "mp"),
            P(None, "dp", "mp"),
            P(None, "dp", "mp"),
            P("mp", "dp"),
            P("mp", "dp"),
            P("mp", "dp"),
            P("dp", "mp"),
            P("dp", "mp"),
            P("dp", "mp"),
            P("mp", "dp"),
            P("mp", "dp"),
            P("mp", "dp"),
            P(None, "dp"),
            P(None, "dp"),
            P(None, "dp"),
        ),
        check_vma=False,
    )
```

profile of v0, /device:TPU:0, one launch (start us, length us, event | category | flops | bytes accessed | tf_op | source)
XLA Modules:
  0.0 857.1 jit_solution(12024804804781086329)
XLA Ops:
  12.4 35.6 %all_gather.16 = bf16[192,768]{0,1:T(8,128)(2,1)} all-gather(bf16[192,96]{0,1:T(8,128)(2,1)S(1)} %copy.141), channel_id=1, replica_groups=mesh['dp'=8,'mp'=4] {'dp'}, dimensions={1}, use_global_device_ids=true | all-gather | bytes 331776 | tf_op jit(solution)/shard_map/all_gather | solution.py:162
  48.0 13.4 %fusion.81 = (bf16[1536,192]{1,0:T(8,128)(2,1)}, bf16[1536,192]{1,0:T(8,128)(2,1)}, bf16[1536,192]{1,0:T(8,128)(2,1)}, bf16[1536,192]{1,0:T(8,128)(2,1)}) fusion(f32[192]{0:T(256)S(1)} %multiply_exponential_fusion, f32[1536]{0:T(1024)S(1)} %get-tuple-element.356, f32[1536]{0:T(1024)S(1)} %get-tuple-element.357), kind=kLoop, calls=%fused_computation.149 | loop fusion | flops 1769472 | bytes 2372352 | tf_op jit(solution)/shard_map/convert.2
  61.5 14.4 %all-gather.5.cloned.1.call-done = bf16[5,768,192]{2,0,1:T(8,128)(2,1)} async-done(((bf16[5,96,192]{2,0,1:T(8,128)(2,1)}), bf16[5,768,192]{2,0,1:T(8,128)(2,1)}) %all-gather.5.cloned.1.call-update) | async-done | bytes 1474576 | tf_op jit(solution)/shard_map/all_gather | solution.py:161
  88.8 3.6 slice.79
  113.3 22.9 %while.32 = (s32[]{:T(128)}, bf16[3,512,3,64]{1,3,2,0:T(8,128)(2,1)}, f32[3,3,512,1]{2,1,3,0:T(4,128)}, f32[3,3,512,1]{2,1,3,0:T(4,128)}, bf16[3,512,3,64]{1,3,2...) while((s32[]{:T(128)}, ...), condition=%wide.region_3.4_spmd, body=%wide.region_0.3_spmd.sunk | while | flops 416773632 | bytes 13309061 | solution.py:191
  146.0 26.1 %all-gather = f32[8,96,4]{1,2,0:T(4,128)S(1)} all-gather(f32[1,96,4]{1,2,0:T(4,128)} %bitcast.203), channel_id=1, replica_groups=mesh['dp'=8,'mp'=4] {'dp'}, dimensions={0}, use_global_device_ids=true | all-gather | bytes 13824 | tf_op jit(solution)/shard_map/all_gather | solution.py:166
  174.3 22.4 %all-reduce.7.cloned.1.call-done = bf16[1536,768]{1,0:T(8,128)(2,1)} async-done(((bf16[1536,768]{1,0:T(8,128)(2,1)}), bf16[1536,768]{1,0:T(8,128)(2,1)}) %all-reduce.7.cloned.1.call-update) | async-done | bytes 2359312 | tf_op jit(solution)/shard_map/psum | solution.py:193
  201.0 39.7 %all-gather.7.cloned.1.call-done = bf16[768,768]{1,0:T(8,128)(2,1)} async-done(((bf16[96,768]{1,0:T(8,128)(2,1)}), bf16[768,768]{1,0:T(8,128)(2,1)}) %all-gather.7.cloned.1.call-update) | async-done | bytes 1179664 | tf_op jit(solution)/shard_map/all_gather | solution.py:163
  240.7 15.5 %multiply_convert_fusion.1 = (bf16[1536,768]{1,0:T(8,128)(2,1)}, f32[1536,768]{1,0:T(8,128)}, f32[1536,768]{1,0:T(8,128)}) fusion(bf16[768,768]{1,0:T(8,128)(2,1)} %all-gather.7.cloned.1.call-done, f32[768]{0:T(1024)} %get-tuple-element.354, f32[768]{0:T(1024)} %get-tuple-element.355, f32[1536]{0:T(1024)S(1)} %fusion.99, ...), kind=kOutput, calls=%fused_computation.110 | convolution fusion | flops 1898053632 | bytes 17713152 | tf_op jit(solution)/shard_map/dot_general | solution.py:199
  256.2 26.9 %all-gather.9.cloned.1.call-done = bf16[768,768]{0,1:T(8,128)(2,1)} async-done(((bf16[768,96]{0,1:T(8,128)(2,1)}), bf16[768,768]{0,1:T(8,128)(2,1)}) %all-gather.9.cloned.1.call-update) | async-done | bytes 1179664 | tf_op jit(solution)/shard_map/all_gather | solution.py:164
  283.1 5.4 convolution_convert_fusion.1
  288.8 54.4 %all-reduce.9.cloned.1.call-done = bf16[1536,768]{1,0:T(8,128)(2,1)} async-done(((bf16[1536,768]{1,0:T(8,128)(2,1)}), bf16[1536,768]{1,0:T(8,128)(2,1)}) %all-reduce.9.cloned.1.call-update) | async-done | bytes 2359312 | tf_op jit(solution)/shard_map/psum | solution.py:202
  343.2 3.8 fusion.121
  363.5 6.8 fusion.104
  370.4 4.2 fusion.107
  374.6 44.7 %all-reduce.11.cloned.1.call-done = bf16[1536,768]{1,0:T(8,128)(2,1)} async-done(((bf16[1536,768]{1,0:T(8,128)(2,1)}), bf16[1536,768]{1,0:T(8,128)(2,1)}) %all-reduce.11.cloned.1.call-update) | async-done | bytes 2359312 | tf_op jit(solution)/shard_map/psum | solution.py:216
  419.3 7.1 multiply_reduce_fusion.1
  426.5 4.8 fusion.119
  444.0 39.6 %while.33 = (s32[]{:T(128)}, bf16[3,512,3,64]{1,3,2,0:T(8,128)(2,1)}, bf16[3,512,3,64]{1,3,2,0:T(8,128)(2,1)}, bf16[3,512,3,64]{1,3,2,0:T(8,128)(2,1)}, bf16[3,5...) while((s32[]{:T(128)}, ...), condition=%wide.region_17.18_spmd, body=%wide.region_15.17_spmd.sunk | while | flops 1124367360 | bytes 33222332 | solution.py:224
  505.3 5.2 bitcast_convert_fusion
  520.9 37.1 %psum.71 = f32[4,768]{1,0:T(4,128)S(1)} all-reduce(f32[4,768]{1,0:T(4,128)S(1)} %pad_maximum_fusion.8), channel_id=1, replica_groups=mesh['dp'=8,'mp'=4] {'dp'}, use_global_device_ids=true, to_apply=%region_27.28 | all-reduce | flops 3072 | bytes 24576 | tf_op jit(solution)/shard_map/psum | solution.py:248
  558.7 7.7 all-reduce.13.cloned.1.call-done
  566.4 5.8 convert_add_fusion
  572.1 266.9 %all-reduce.15.cloned.1.call-done = (f32[5,768,192]{1,2,0:T(8,128)}, f32[192,768]{1,0:T(8,128)}, f32[768,768]{1,0:T(8,128)}, f32[768,768]{0,1:T(8,128)}) async-done(((f32[5,768,192]{1,2,0:T(8,128)}, f32[192,768]{1,0:T(8,128)}, f32[768,768]{1,0:T(8,128)}, f32[768,768]{0,1:T(8,128)}), (f32[5,768,192]{1,2,0:T(8,128)}, f32[192,768]{1,0:T(8,128)}, f32[768,768]{1,0:T(8,128)}, ...) | async-done | bytes 8257552 | tf_op jit(solution)/shard_map/psum | solution.py:248
  (286 shorter events, 190.2 us)
Async XLA Ops:
  7.2 68.7 %all-gather.5.cloned.1.call-start = ((), (), s32[]{:S(2)}) async-start(), calls=%async_computation | async-start | bytes 3538944 | tf_op jit(solution)/shard_map/all_gather | solution.py:161
  9.2 187.5 %all-reduce.7.cloned.1.call-start = ((), (), s32[]{:S(2)}) async-start(), calls=%async_computation.1 | async-start | bytes 4718592 | tf_op jit(solution)/shard_map/psum | solution.py:193
  85.0 10.9 %copy-start.1 = (bf16[1536,768]{1,0:T(8,128)(2,1)S(1)}, bf16[1536,768]{1,0:T(8,128)(2,1)}, u32[]{:S(2)}) copy-start(bf16[1536,768]{1,0:T(8,128)(2,1)} %param.24) | copy-start | bytes 7077892
  136.2 9.7 %copy-start.18 = (s32[3,512]{1,0:T(4,128)}, s32[3,512]{1,0:T(4,128)S(1)}, u32[]{:S(2)}) copy-start(s32[3,512]{1,0:T(4,128)S(1)} %get-tuple-element.785) | copy-start | bytes 18436
  136.2 9.7 %copy-start.19 = (s32[3,512]{1,0:T(4,128)}, s32[3,512]{1,0:T(4,128)S(1)}, u32[]{:S(2)}) copy-start(s32[3,512]{1,0:T(4,128)S(1)} %get-tuple-element.786) | copy-start | bytes 18436
  142.1 98.6 %all-gather.7.cloned.1.call-start = ((), (), s32[]{:S(2)}) async-start(), calls=%async_computation.2 | async-start | bytes 1327104 | tf_op jit(solution)/shard_map/all_gather | solution.py:163
  144.2 138.9 %all-gather.9.cloned.1.call-start = ((), (), s32[]{:S(2)}) async-start(), calls=%async_computation.3 | async-start | bytes 1327104 | tf_op jit(solution)/shard_map/all_gather | solution.py:164
  146.0 197.2 %all-reduce.9.cloned.1.call-start = ((), (), s32[]{:S(2)}) async-start(), calls=%async_computation.4 | async-start | bytes 4718592 | tf_op jit(solution)/shard_map/psum | solution.py:202
  288.6 130.7 %all-reduce.11.cloned.1.call-start = ((), (), s32[]{:S(2)}) async-start(), calls=%async_computation.5 | async-start | bytes 4718592 | tf_op jit(solution)/shard_map/psum | solution.py:216
  363.4 202.9 %all-reduce.13.cloned.1.call-start = ((), (), s32[]{:S(2)}) async-start(), calls=%async_computation.6 | async-start | bytes 4718592 | tf_op jit(solution)/shard_map/psum | solution.py:238
  419.3 7.1 copy-start.25
  419.3 7.1 copy-start.4
  419.3 7.1 copy-start.7
  419.3 7.1 copy-start.23
  419.3 7.1 copy-start.27
  510.5 328.5 %all-reduce.15.cloned.1.call-start = ((), (), s32[]{:S(2)}) async-start(), calls=%async_computation.7 | async-start | bytes 16515072 | tf_op jit(solution)/shard_map/psum | solution.py:248
  519.2 38.9 %copy-start.35 = (f32[4,96]{1,0:T(4,128)S(1)}, f32[4,96]{1,0:T(4,128)}, u32[]{:S(2)}) copy-start(f32[4,96]{1,0:T(4,128)} %param.41) | copy-start | bytes 4612
  519.2 38.8 %copy-start.36 = (f32[4,96]{1,0:T(4,128)S(1)}, f32[4,96]{1,0:T(4,128)}, u32[]{:S(2)}) copy-start(f32[4,96]{1,0:T(4,128)} %param.42) | copy-start | bytes 4612
  519.2 38.8 %copy-start.37 = (f32[4,96]{1,0:T(4,128)S(1)}, f32[4,96]{1,0:T(4,128)}, u32[]{:S(2)}) copy-start(f32[4,96]{1,0:T(4,128)} %param.43) | copy-start | bytes 4612
  572.1 271.6 %copy-start.12 = (f32[768,96]{0,1:T(8,128)S(1)}, f32[768,96]{0,1:T(8,128)}, u32[]{:S(2)}) copy-start(f32[768,96]{0,1:T(8,128)} %param.38) | copy-start | bytes 884740
  572.1 273.8 %copy-start.13 = (f32[96,768]{1,0:T(8,128)S(1)}, f32[96,768]{1,0:T(8,128)}, u32[]{:S(2)}) copy-start(f32[96,768]{1,0:T(8,128)} %param.35) | copy-start | bytes 884740
  840.6 7.4 copy-start.16
  840.7 7.4 copy-start.20
  840.7 7.4 copy-start.21
  (32 other events, 110.7 us)
Sparse Core Ops, SparseCore 0:
  10.8 65.0 all-gather.4
  142.2 54.5 all-reduce.6
  199.5 41.1 all-gather.6
  243.3 39.8 all-gather.8
  288.7 54.4 all-reduce.8
  363.6 55.7 all-reduce.10
  510.6 55.7 all-reduce.12
  570.8 268.1 all-reduce.14
where the time goes:
time: 869 us; the launch traced here: 857 us
  waiting for transfers between devices  477 us (55%)
  local copies, waits for them, and re-layouts  101 us (12%)
  blocking collectives  98.8 us (11%)
  matrix products  91.3 us (11%)
  other arithmetic  72.2 us (8%)
  between operations  15.3 us (2%)
    psum x1, waiting for transfers between devices, per_device(): summed = lax.psum((grad_in, grad_out, grad_up, grad_down, grad_norm), 'dp')  267 us
    psum x1, waiting for transfers between devices, per_device(): lax.psum(jnp.dot(active, weight_down, preferred_element_type=jnp.float32)...  54.4 us
    psum x1, waiting for transfers between devices, per_device(): lax.psum(ffn_back_term.astype(jnp.bfloat16), 'mp').astype(jnp.float32)  44.7 us
    all_gather x1, waiting for transfers between devices, per_device(): lax.all_gather(ffn_in.astype(jnp.bfloat16), 'dp', axis=0, tiled=True)  39.7 us
    psum x1, blocking collectives, per_device(): summed = lax.psum((grad_in, grad_out, grad_up, grad_down, grad_norm), 'dp')  37.1 us
    all_gather x1, blocking collectives, per_device(): lax.all_gather(attn_out.astype(jnp.bfloat16), 'dp', axis=1, tiled=True)  35.6 us
    all_gather x1, waiting for transfers between devices, per_device(): lax.all_gather(ffn_out.astype(jnp.bfloat16), 'dp', axis=1, tiled=True)  26.9 us
    all_gather x1, blocking collectives, per_device(): norm_full = lax.all_gather(norm_weight, 'dp', axis=1, tiled=True)  26.1 us
  transfers between devices with their start and end apart: 8, of which 8 were waited for; matrix products, arithmetic and copies ran while one was open for 8% of the time, Pallas kernels for 0%

commit v1 on v0

v1 whole, which is shorter than its diff:
```python
from functools import partial
import math

import jax
import jax.numpy as jnp
from jax import lax
from jax.experimental import pallas as pl
from jax.experimental.pallas import tpu as pltpu
from jax.sharding import PartitionSpec as P

D = 768
HEAD_DIM = 64
SEQ = 512
HALF = SEQ // 2
STEP = 10
HEADS = 3
QK = HEADS * 128
ATT = 3 * QK
FFN = 2 * D

epsilon_norm = 1e-12
epsilon_adam = 1e-08
beta_first = 0.9
beta_second = 0.999
rate_matrix = 0.05
rate_norm = 0.2
decay_matrix = 0.01
masked_score = -1e30

F32 = jnp.float32
BF16 = jnp.bfloat16
VMEM_LIMIT = 60 * 1024 * 1024


def dot(a, b):
    return jnp.dot(a, b, preferred_element_type=F32)


def dot_nt(a, b):
    return lax.dot_general(a, b, (((1,), (1,)), ((), ())), preferred_element_type=F32)


def dot_tn(a, b):
    return lax.dot_general(a, b, (((0,), (0,)), ((), ())), preferred_element_type=F32)


def remote(src, dst, send, recv, device):
    return pltpu.make_async_remote_copy(
        src_ref=src,
        dst_ref=dst,
        send_sem=send,
        recv_sem=recv,
        device_id=device,
        device_id_type=pl.DeviceIdType.MESH,
    )


def steps(total, size, body):
    def run(i, carry):
        body(pl.multiple_of(i * size, size))
        return carry

    lax.fori_loop(0, total // size, run, 0)


def lower_half(shape):
    return lax.broadcasted_iota(jnp.int32, shape, len(shape) - 1) % 128 < HEAD_DIM


class Place:
    def __init__(self, ring):
        self.dp = lax.axis_index("dp")
        self.mp = lax.axis_index("mp")
        self.half = self.mp % 2
        self.pair = (self.dp, self.mp + 1 - 2 * self.half)
        self.across = (self.dp, (self.mp + 2) % 4)
        self.ring = ring
        self.z = self.dp // 2
        self.x = self.dp % 2
        self.xdev = (self.dp + 1 - 2 * self.x, self.mp)

    def zdev(self, k):
        return (((self.z + k) % self.ring) * 2 + self.x, self.mp)

    def came(self, k):
        return ((self.z + self.ring - k) % self.ring) * 2 + self.x

    def came_other(self, k):
        return ((self.z + self.ring - k) % self.ring) * 2 + 1 - self.x

    def greet(self):
        peers = [self.pair, self.across]
        if self.ring:
            peers += [self.xdev] + [self.zdev(k) for k in range(1, self.ring)]
        barrier = pltpu.get_barrier_semaphore()
        for peer in peers:
            pl.semaphore_signal(
                barrier, inc=1, device_id=peer, device_id_type=pl.DeviceIdType.MESH
            )
        pl.semaphore_wait(barrier, len(peers))

    def own(self, r):
        return pl.ds(pl.multiple_of(r * SEQ + self.half * HALF, HALF), HALF)

    def other(self, r):
        return pl.ds(pl.multiple_of(r * SEQ + (1 - self.half) * HALF, HALF), HALF)


class Gather:
    def __init__(self, place, kind, src, at, sems):
        self.p, self.src, self.at = place, src, at
        zs, zr, xs, xr = sems
        self.zs, self.zr, self.xs, self.xr = (
            zs.at[kind],
            zr.at[kind],
            xs.at[kind],
            xr.at[kind],
        )

    def along(self, k):
        p = self.p
        return remote(self.src, self.at(p.dp), self.zs.at[k], self.zr.at[k], p.zdev(k))

    def onward(self, k):
        p = self.p
        src = self.src if k == 0 else self.at(p.came(k))
        return remote(src, self.at(p.came(k)), self.xs.at[k], self.xr.at[k], p.xdev)

    def start(self):
        for k in range(1, self.p.ring):
            self.along(k).start()
        self.onward(0).start()

    def forward(self):
        p = self.p
        for k in range(1, p.ring):
            remote(
                self.src, self.at(p.came(k)), self.zs.at[k], self.zr.at[k], p.zdev(k)
            ).wait_recv()
            self.onward(k).start()

    def finish(self):
        p = self.p
        for k in range(p.ring):
            remote(
                self.src, self.at(p.came_other(k)), self.xs.at[k], self.xr.at[k], p.xdev
            ).wait_recv()
        for k in range(1, p.ring):
            self.along(k).wait_send()
        for k in range(p.ring):
            self.onward(k).wait_send()


class Sum:
    def __init__(self, place, parity, psend, precv, sums, yrecv, sems):
        self.p = place
        self.psend, self.precv = psend, precv
        self.sums, self.yrecv = sums.at[parity], yrecv.at[parity]
        ps, pr, ys, yr = sems
        self.ps, self.pr, self.ys, self.yr = (
            ps.at[parity],
            pr.at[parity],
            ys.at[parity],
            yr.at[parity],
        )

    def to_pair(self, r):
        return remote(
            self.psend.at[r], self.precv.at[r], self.ps.at[r], self.pr.at[r], self.p.pair
        )

    def over(self, r):
        return remote(
            self.sums.at[r], self.yrecv.at[r], self.ys.at[r], self.yr.at[r], self.p.across
        )

    def give(self, r, value):
        self.psend[r] = value.astype(BF16)
        self.to_pair(r).start()

    def keep(self, r, value):
        self.to_pair(r).wait_recv()
        self.sums[r] = (value + self.precv[r].astype(F32)).astype(BF16)
        self.over(r).start()

    def wait(self, r):
        self.over(r).wait_recv()

    def total(self, r, rows):
        return self.sums[r, rows, :].astype(F32) + self.yrecv[r, rows, :].astype(F32)

    def sent(self, r):
        self.to_pair(r).wait_send()

    def close(self, r):
        self.over(r).wait_send()


def rolled(value):
    return pltpu.roll(value.astype(F32), HEAD_DIM, 1)


def embed_rows(coords, lanes, out, row):
    rows = pl.ds(row, 32)
    here = coords[rows, :]
    across, upward = here[:, 0:1], here[:, 1:2]
    frequency, second, shift = lanes[0:1, :], lanes[1:2, :], lanes[2:3, :]
    angle = (across + (upward - across) * second) * frequency
    turns = jnp.round(angle * (2.0 / math.pi))
    rest = ((angle - turns * 1.5703125) - turns * 4.837512969970703125e-4) - turns * (
        7.54978995489188216e-8
    )
    square = rest * rest
    sine = rest + rest * square * (
        -1.6666654611e-1 + square * (8.3321608736e-3 + square * -1.9515295891e-4)
    )
    cosine = (
        1.0
        - 0.5 * square
        + square
        * square
        * (
            4.166664568298827e-2
            + square * (-1.388731625493765e-3 + square * 2.443315711809948e-5)
        )
    )
    quarter = (turns + shift).astype(jnp.int32)
    value = jnp.where((quarter & 1) == 1, cosine, sine)
    out[rows, :] = jnp.where((quarter & 2) == 2, -value, value).astype(BF16)


def attend_kernel(
    ring,
    chunks,
    hidden,
    cols,
    keyrow,
    lanes,
    packa,
    packf,
    pnorm,
    wtx,
    wop,
    wf,
    nbuf,
    lq,
    rk,
    vk,
    probs,
    ctx,
    emb,
    total,
    wa,
    scores,
    psend,
    precv,
    sums,
    yrecv,
    zs,
    zr,
    xs,
    xr,
    ps,
    pr,
    ys,
    yr,
):
    p = Place(ring)
    p.greet()
    sems = (zs, zr, xs, xr)
    if ring:
        share = packa.shape[0]

        def rows_of(ref):
            return lambda d: ref.at[pl.ds(pl.multiple_of(d * share, share), share), :]

        gather_a = Gather(p, 0, packa, rows_of(wa), sems)
        gather_f = Gather(p, 1, packf, rows_of(wf), sems)
        gather_n = Gather(p, 2, pnorm, lambda d: nbuf.at[d], sems)
        gather_a.start()
        gather_n.start()
        mine = pl.ds(pl.multiple_of(p.dp * share, share), share)
        wa[mine, :] = packa[...]
        wf[mine, :] = packf[...]
        nbuf[p.dp] = pnorm[...]
    else:
        wa[...] = packa[...]
    tokens = hidden.shape[0]
    steps(tokens, 32, partial(embed_rows, cols, lanes, emb))
    if ring:
        gather_a.forward()
        gather_n.forward()
        gather_a.finish()
        gather_n.finish()
        gather_f.start()

    def build(row):
        rows = pl.ds(row, 128)
        low = lower_half((128, 128))
        wtx[rows, :QK] = wa[rows, :QK]
        for h in range(HEADS):
            qk_cols = slice(h * 128, (h + 1) * 128)
            ov_cols = slice(QK + h * 128, QK + (h + 1) * 128)
            ov = wa[rows, ov_cols].astype(F32)
            wtx[rows, ov_cols] = jnp.where(low, rolled(wa[rows, qk_cols]), ov).astype(BF16)
            wop[rows, qk_cols] = jnp.where(low, 0.0, rolled(ov)).astype(BF16)

    steps(D, 128, build)

    def project(row):
        rows = pl.ds(row, HALF)
        text = dot(hidden[rows, :], wtx[...])
        box = dot(emb[rows, :], wa[:, 2 * QK :])
        low = lower_half((HALF, QK))
        lq[rows, :] = jnp.where(low, text[:, :QK], box).astype(BF16)
        rk[rows, :] = jnp.where(low, box, text[:, :QK]).astype(BF16)
        vk[rows, :] = text[:, QK:].astype(BF16)

    steps(tokens, HALF, project)
    reduce = Sum(p, 0, psend, precv, sums, yrecv, (ps, pr, ys, yr))

    def attend(r, side):
        start = side * HALF
        q_rows = pl.ds(pl.multiple_of(r * SEQ + start, HALF), HALF)
        k_rows = pl.ds(pl.multiple_of(r * SEQ, SEQ), SEQ)
        low = lower_half((HALF, 128))
        for h in range(HEADS):
            tile = slice(h * 128, (h + 1) * 128)
            left = lq[q_rows, tile]
            both = jnp.concatenate([left, jnp.where(low, left, jnp.zeros_like(left))], axis=1)
            right = jnp.concatenate([rk[k_rows, tile], vk[k_rows, tile]], axis=1)
            scores[...] = dot_nt(both, right)

            def softmax(row):
                rows = pl.ds(row, 32)
                pages = cols[pl.ds(r * SEQ + start + row, 32), 2:3]
                here = lax.broadcasted_iota(jnp.int32, (32, SEQ), 0) + (start + row)
                there = lax.broadcasted_iota(jnp.int32, (32, SEQ), 1)
                allowed = (pages == keyrow[r]) | (here == there)
                value = jnp.where(allowed, scores[rows, :] * HEAD_DIM**-0.5, masked_score)
                raised = jnp.exp(value - jnp.max(value, axis=-1, keepdims=True))
                value = raised / jnp.sum(raised, axis=-1, keepdims=True)
                probs[r, h, pl.ds(pl.multiple_of(start + row, 32), 32), :] = value.astype(BF16)

            steps(HALF, 32, softmax)
            found = dot(
                probs[r, h, pl.ds(pl.multiple_of(start, HALF), HALF), :], vk[k_rows, tile]
            )
            ctx[q_rows, tile] = jnp.where(low, pltpu.roll(found, HEAD_DIM, 1), 0.0).astype(BF16)
        return dot_nt(ctx[q_rows, :], wa[:, QK : 2 * QK])

    def chunk(r, carry):
        reduce.give(r, attend(r, 1 - p.half))
        reduce.keep(r, attend(r, p.half))
        return carry

    lax.fori_loop(0, chunks, chunk, 0)
    if ring:
        gather_f.forward()

    def collect(r, carry):
        reduce.wait(r)
        total[r] = reduce.total(r, slice(None))
        reduce.sent(r)
        reduce.close(r)
        return carry

    lax.fori_loop(0, chunks, collect, 0)
    if ring:
        gather_f.finish()


def norm_of(values):
    center = jnp.mean(values, axis=-1, keepdims=True)
    shifted = values - center
    spread = jnp.mean(shifted * shifted, axis=-1, keepdims=True)
    scale = lax.rsqrt(spread + epsilon_norm)
    return shifted * scale, scale


def norm_back(upstream, normal, scale):
    first = jnp.mean(upstream, axis=-1, keepdims=True)
    second = jnp.mean(upstream * normal, axis=-1, keepdims=True)
    return (upstream - first - normal * second) * scale


def fold(values):
    rows, width = values.shape
    return jnp.sum(values.reshape(rows // 8, 8, width), axis=0)


def forward_kernel(
    chunks,
    attn,
    hidden,
    out_grad,
    norm,
    wf,
    mixed,
    gtwo,
    xone,
    rone,
    tback,
    gup,
    gdown,
    ngrad,
    shared,
    active,
    slope,
    low_two,
    pre,
    stage,
    psend,
    precv,
    sums,
    yrecv,
    ss,
    sr,
    gs,
    gr,
    ms,
    mr,
    ml,
    ps,
    pr,
    ys,
    yr,
):
    p = Place(0)
    p.greet()
    gain_one, bias_one = norm[0:1, :], norm[1:2, :]
    gain_two, bias_two = norm[2:3, :], norm[3:4, :]

    def share_one(rows, r):
        view = shared.at[rows, :]
        return remote(view, view, ss.at[r], sr.at[r], p.pair)

    def share_two(rows, r):
        view = low_two.at[rows, :]
        return remote(view, view, gs.at[r], gr.at[r], p.pair)

    def first_norm(r, carry):
        base = r * SEQ + p.half * HALF

        def part(row):
            rows = pl.ds(pl.multiple_of(base + row, 32), 32)
            here = pl.ds(row, 32)
            normal, scale = norm_of(hidden[rows, :].astype(F32) + attn[r, here, :])
            xone[r, here, :] = normal
            rone[r, here, :] = jnp.broadcast_to(scale, (32, 128))
            shared[rows, :] = (normal * gain_one + bias_one).astype(BF16)

        steps(HALF, 32, part)
        share_one(p.own(r), r).start()
        return carry

    lax.fori_loop(0, chunks, first_norm, 0)
    first = Sum(p, 0, psend, precv, sums, yrecv, (ps, pr, ys, yr))
    second = Sum(p, 1, psend, precv, sums, yrecv, (ps, pr, ys, yr))

    def up_down(rows_at):
        rows = pl.ds(rows_at, HALF)
        pre[...] = dot(shared[rows, :], wf[:, :D])

        def gelu(row):
            here = pl.ds(row, 16)
            there = pl.ds(pl.multiple_of(rows_at + row, 16), 16)
            value = pre[here, :]
            below = 0.5 + 0.5 * lax.erf(value * math.sqrt(0.5))
            active[there, :] = (value * below).astype(BF16)
            density = jnp.exp(-0.5 * value * value) * (1.0 / math.sqrt(2.0 * math.pi))
            slope[there, :] = (below + value * density).astype(BF16)

        steps(HALF, 16, gelu)
        return dot_nt(active[rows, :], wf[:, D:])

    def feed(r, carry):
        share_one(p.other(r), r).wait_recv()
        first.give(r, up_down(pl.multiple_of(r * SEQ + (1 - p.half) * HALF, HALF)))
        first.keep(r, up_down(pl.multiple_of(r * SEQ + p.half * HALF, HALF)))
        return carry

    lax.fori_loop(0, chunks, feed, 0)
    ngrad[...] = jnp.zeros_like(ngrad)

    def mixed_here(r):
        return pltpu.make_async_copy(stage.at[r], mixed.at[p.own(r), :], ml.at[r])

    def mixed_pair(rows, r):
        return remote(stage.at[r], mixed.at[rows, :], ms.at[r], mr.at[r], p.pair)

    def back(rows_at):
        rows = pl.ds(rows_at, HALF)
        pre[...] = dot(low_two[rows, :], wf[:, D:])

        def times(row):
            here = pl.ds(row, 32)
            there = pl.ds(pl.multiple_of(rows_at + row, 32), 32)
            slope[there, :] = (pre[here, :] * slope[there, :].astype(F32)).astype(BF16)

        steps(HALF, 32, times)
        return dot_nt(slope[rows, :], wf[:, :D])

    def turn(r, carry):
        first.wait(r)
        base = r * SEQ + p.half * HALF

        def part(row):
            rows = pl.ds(pl.multiple_of(base + row, 32), 32)
            here = pl.ds(row, 32)
            residual = xone[r, here, :] * gain_one + bias_one + first.total(r, here)
            normal, scale = norm_of(residual)
            stage[r, here, :] = (normal * gain_two + bias_two).astype(BF16)
            grad = out_grad[rows, :].astype(F32)
            value = norm_back(grad * gain_two, normal, scale)
            gtwo[r, here, :] = value
            low_two[rows, :] = value.astype(BF16)
            ngrad[0:8, :] += fold(grad * normal)
            ngrad[8:16, :] += fold(grad)

        steps(HALF, 32, part)
        share_two(p.own(r), r).start()
        mixed_here(r).start()
        mixed_pair(p.own(r), r).start()
        share_two(p.other(r), r).wait_recv()
        first.sent(r)
        second.give(r, back(pl.multiple_of(r * SEQ + (1 - p.half) * HALF, HALF)))
        second.keep(r, back(pl.multiple_of(r * SEQ + p.half * HALF, HALF)))
        return carry

    lax.fori_loop(0, chunks, turn, 0)

    def weights(row):
        rows = pl.ds(row, 128)
        gup[rows, :] = dot_tn(shared[:, rows], slope[...])
        gdown[rows, :] = dot_tn(low_two[:, rows], active[...])

    steps(D, 128, weights)

    def collect(r, carry):
        second.wait(r)
        tback[r] = second.total(r, slice(None))
        second.sent(r)
        first.close(r)
        second.close(r)
        share_one(p.own(r), r).wait_send()
        share_two(p.own(r), r).wait_send()
        mixed_here(r).wait()
        mixed_pair(p.own(r), r).wait_send()
        mixed_pair(p.other(r), r).wait_recv()
        return carry

    lax.fori_loop(0, chunks, collect, 0)


class Scatter:
    def __init__(self, place, share, src, xsend, xrecv, zsend, zrecv, sems):
        self.p, self.share, self.src = place, share, src
        self.xsend, self.xrecv, self.zsend, self.zrecv = xsend, xrecv, zsend, zrecv
        self.xs, self.xr, self.zs, self.zr = sems

    def rows(self, k, x):
        d = ((self.p.z + k) % self.p.ring) * 2 + x
        return pl.ds(pl.multiple_of(d * self.share, self.share), self.share)

    def xcopy(self, k):
        return remote(
            self.xsend.at[k], self.xrecv.at[k], self.xs.at[k], self.xr.at[k], self.p.xdev
        )

    def zcopy(self, k):
        return remote(
            self.zsend.at[k], self.zrecv.at[k], self.zs.at[k], self.zr.at[k], self.p.zdev(k)
        )

    def order(self):
        return list(range(1, self.p.ring)) + [0]

    def start(self):
        for k in self.order():
            self.xsend[k] = self.src[self.rows(k, 1 - self.p.x), :].astype(BF16)
            self.xcopy(k).start()

    def middle(self):
        for k in range(1, self.p.ring):
            self.xcopy(k).wait_recv()
            value = self.src[self.rows(k, self.p.x), :] + self.xrecv[k].astype(F32)
            self.zsend[k] = value.astype(BF16)
            self.zcopy(k).start()

    def finish(self, out):
        self.xcopy(0).wait_recv()
        value = self.src[self.rows(0, self.p.x), :] + self.xrecv[0].astype(F32)
        for k in range(1, self.p.ring):
            self.zcopy(k).wait_recv()
            value = value + self.zrecv[k].astype(F32)
        out[...] = value
        for k in range(self.p.ring):
            self.xcopy(k).wait_send()
        for k in range(1, self.p.ring):
            self.zcopy(k).wait_send()


def backward_kernel(
    ring,
    chunks,
    tback,
    gtwo,
    xone,
    rone,
    norm,
    lq,
    rk,
    vk,
    probs,
    ctx,
    hidden,
    emb,
    wtx,
    wop,
    gup,
    gdown,
    ntwo,
    igrad,
    outa,
    outup,
    outdown,
    nout,
    low_one,
    gone,
    gtext,
    gbox,
    gscore,
    gctx,
    dprob,
    ga,
    stage,
    psend,
    precv,
    sums,
    yrecv,
    nbuf,
    nrecv,
    *rest,
):
    scatters, rest = rest[:12], rest[12:]
    (gs, gr, ims, imr, iml, ps, pr, ys, yr, ns, nr), rest = rest[:11], rest[11:]
    p = Place(ring)
    p.greet()
    gain_one = norm[0:1, :]
    if ring:
        share = outup.shape[0]
        up = Scatter(p, share, gup, *scatters[0:4], [s.at[0] for s in rest])
        down = Scatter(p, share, gdown, *scatters[4:8], [s.at[1] for s in rest])
        att = Scatter(p, share, ga, *scatters[8:12], [s.at[2] for s in rest])
        up.start()
        down.start()
    nbuf[0:16, :] = jnp.zeros((16, D), F32)
    nbuf[16:32, :] = ntwo[...]

    def share_one(rows, r):
        view = low_one.at[rows, :]
        return remote(view, view, gs.at[r], gr.at[r], p.pair)

    def first_norm(r, carry):
        base = r * SEQ + p.half * HALF

        def part(row):
            rows = pl.ds(pl.multiple_of(base + row, 32), 32)
            here = pl.ds(row, 32)
            grad = gtwo[r, here, :] + tback[r, here, :]
            normal = xone[r, here, :]
            value = norm_back(grad * gain_one, normal, rone[r, here, 0:1])
            gone[r, here, :] = value
            low_one[rows, :] = value.astype(BF16)
            nbuf[0:8, :] += fold(grad * normal)
            nbuf[8:16, :] += fold(grad)

        steps(HALF, 32, part)
        share_one(p.own(r), r).start()
        return carry

    lax.fori_loop(0, chunks, first_norm, 0)
    for row in range(4):
        nbuf[row : row + 1, :] = jnp.sum(nbuf[row * 8 : row * 8 + 8, :], axis=0, keepdims=True)
    if ring:
        norm_pair = remote(nbuf.at[0:8], nrecv.at[0], ns.at[0], nr.at[0], p.pair)
        norm_pair.start()
    reduce = Sum(p, 0, psend, precv, sums, yrecv, (ps, pr, ys, yr))
    score_scale = HEAD_DIM**-0.5

    def attend(r):
        k_rows = pl.ds(pl.multiple_of(r * SEQ, SEQ), SEQ)
        for side in range(2):
            rows = pl.ds(pl.multiple_of(r * SEQ + side * HALF, HALF), HALF)
            gctx[side * HALF : (side + 1) * HALF, :] = dot(low_one[rows, :], wop[...]).astype(BF16)
        low = lower_half((SEQ, 128))
        for h in range(HEADS):
            tile = slice(h * 128, (h + 1) * 128)
            right_v = vk[k_rows, tile]
            right_k = rk[k_rows, tile]
            dprob[...] = dot_nt(gctx[:, tile], right_v)

            def soften(row):
                rows = pl.ds(row, 32)
                grad = dprob[rows, :]
                prob = probs[r, h, rows, :].astype(F32)
                weighted = jnp.sum(prob * grad, axis=-1, keepdims=True)
                gscore[rows, :] = (prob * (grad - weighted)).astype(BF16)

            steps(SEQ, 32, soften)
            left = dot(gscore[...], right_k) * score_scale
            right = dot_tn(gscore[...], lq[k_rows, tile]) * score_scale
            value = dot_tn(probs[r, h], gctx[:, tile])
            gtext[k_rows, tile] = jnp.where(
                low, left + pltpu.roll(left, HEAD_DIM, 1), right + pltpu.roll(right, HEAD_DIM, 1)
            ).astype(BF16)
            gbox[k_rows, tile] = jnp.where(low, right, left).astype(BF16)
            gtext[k_rows, QK + h * 128 : QK + (h + 1) * 128] = value.astype(BF16)

    def partial_of(rows):
        return dot_nt(gtext[rows, :], wtx[...])

    def igrad_here(r):
        return pltpu.make_async_copy(stage.at[r], igrad.at[p.own(r), :], iml.at[r])

    def igrad_pair(rows, r):
        return remote(stage.at[r], igrad.at[rows, :], ims.at[r], imr.at[r], p.pair)

    def chunk(r, carry):
        share_one(p.other(r), r).wait_recv()
        attend(r)
        reduce.give(r, partial_of(p.other(r)))
        reduce.keep(r, partial_of(p.own(r)))
        return carry

    lax.fori_loop(0, chunks, chunk, 0)

    def weights(row):
        rows = pl.ds(row, 128)
        text = dot_tn(hidden[:, rows], gtext[...])
        ga[rows, :QK] = text[:, :QK]
        ga[rows, QK : 2 * QK] = text[:, QK:] + dot_tn(low_one[:, rows], ctx[...])
        ga[rows, 2 * QK :] = dot_tn(emb[:, rows], gbox[...])

    steps(D, 128, weights)
    if ring:
        att.start()
        up.middle()
        down.middle()
        norm_pair.wait_recv()
        nbuf[8:16, :] = nbuf[0:8, :] + nrecv[0]
        norm_x = remote(nbuf.at[8:16], nrecv.at[1], ns.at[1], nr.at[1], p.xdev)
        norm_x.start()
        att.middle()
        norm_x.wait_recv()
        nbuf[16:24, :] = nbuf[8:16, :] + nrecv[1]
        norm_z = [
            remote(nbuf.at[16:24], nrecv.at[1 + k], ns.at[1 + k], nr.at[1 + k], p.zdev(k))
            for k in range(1, ring)
        ]
        for copy in norm_z:
            copy.start()

    def collect(r, carry):
        reduce.wait(r)

        def part(row):
            here = pl.ds(row, 32)
            stage[r, here, :] = gone[r, here, :] + reduce.total(r, here)

        steps(HALF, 32, part)
        igrad_here(r).start()
        igrad_pair(p.own(r), r).start()
        reduce.sent(r)
        reduce.close(r)
        share_one(p.own(r), r).wait_send()
        return carry

    lax.fori_loop(0, chunks, collect, 0)
    if ring:
        up.finish(outup)
        down.finish(outdown)
        att.finish(outa)
        summed = nbuf[16:24, :]
        for k in range(1, ring):
            norm_z[k - 1].wait_recv()
            summed = summed + nrecv[1 + k]
        nout[...] = summed
        for copy in [norm_pair, norm_x] + norm_z:
            copy.wait_send()
    else:
        outa[...] = ga[...]
        nout[...] = nbuf[0:8, :]

    def settle(r, carry):
        igrad_here(r).wait()
        igrad_pair(p.own(r), r).wait_send()
        igrad_pair(p.other(r), r).wait_recv()
        return carry

    lax.fori_loop(0, chunks, settle, 0)


def adam_step(weight, gradient, moment, second, rate, decay):
    moment_new = beta_first * moment + (1.0 - beta_first) * gradient
    second_new = beta_second * second + (1.0 - beta_second) * gradient * gradient
    moment_hat = moment_new / (1.0 - beta_first**STEP)
    second_hat = second_new / (1.0 - beta_second**STEP)
    weight_new = weight - rate * (
        moment_hat / (jnp.sqrt(second_hat) + epsilon_adam) + decay * weight
    )
    return (weight_new, moment_new, second_new)


def vmem():
    return pl.BlockSpec(memory_space=pltpu.VMEM)


def dma(*shape):
    return pltpu.SemaphoreType.DMA(shape)


def sum_scratch(chunks, sums):
    return [pltpu.VMEM((chunks, HALF, D), BF16)] * 2 + [
        pltpu.VMEM((sums, chunks, HALF, D), BF16)
    ] * 2


def params(number):
    return pltpu.CompilerParams(
        collective_id=number, has_side_effects=True, vmem_limit_bytes=VMEM_LIMIT
    )


def interleave(first, second):
    rows = first.shape[0]
    pair = [part.reshape(rows, HEADS, 1, HEAD_DIM) for part in (first, second)]
    return jnp.concatenate(pair, axis=2).reshape(rows, QK)


def split_pair(both):
    rows = both.shape[0]
    pair = both.reshape(rows, HEADS, 2, HEAD_DIM)
    return pair[:, :, 0].reshape(rows, QK // 2), pair[:, :, 1].reshape(rows, QK // 2)


def box_lanes():
    quarter = D // 4
    ladder = jnp.arange(quarter).astype(F32)
    frequency = jnp.exp(ladder * (-math.log(10000.0) / quarter))
    zero, one = jnp.zeros((quarter,), F32), jnp.ones((quarter,), F32)
    return jnp.stack(
        [
            jnp.concatenate([frequency] * 4),
            jnp.concatenate([zero, zero, one, one]),
            jnp.concatenate([zero, one, zero, one]),
        ]
        + [jnp.zeros((D,), F32)] * 5
    )


def per_device(
    devices,
    hidden_in,
    page_ids,
    pad_mask,
    boxes,
    out_grad,
    attn_in,
    attn_in_moment,
    attn_in_second,
    attn_out,
    attn_out_moment,
    attn_out_second,
    ffn_in,
    ffn_in_moment,
    ffn_in_second,
    ffn_out,
    ffn_out_moment,
    ffn_out_second,
    norm_weight,
    norm_moment,
    norm_second,
):
    tokens = hidden_in.shape[0]
    chunks = tokens // SEQ
    share = attn_in.shape[1]
    ring = devices // 2 if share % 16 == 0 else 0
    low_in = attn_in.astype(BF16)
    packa = jnp.concatenate(
        [
            interleave(low_in[0], low_in[1]),
            interleave(attn_out.T.astype(BF16), low_in[2]),
            interleave(low_in[4], low_in[3]),
        ],
        axis=1,
    )
    packf = jnp.concatenate([ffn_in.astype(BF16), ffn_out.T.astype(BF16)], axis=1)
    pnorm = jnp.pad(norm_weight, ((0, 4), (0, -share % 128)))
    if not ring:
        packa = lax.all_gather(packa, "dp", axis=0, tiled=True)
        wf_full = lax.all_gather(packf, "dp", axis=0, tiled=True)
        norm_full = lax.all_gather(norm_weight, "dp", axis=1, tiled=True)
        packf = packf[:16]
    pages = page_ids.astype(F32)
    cols = jnp.stack([boxes[:, 0].astype(F32), boxes[:, 1].astype(F32), pages], axis=1)
    keyrow = jnp.where(pad_mask == 0, pages, -1.0).reshape(chunks, 1, SEQ)
    own = jax.ShapeDtypeStruct((chunks, HALF, D), F32)
    wide = jax.ShapeDtypeStruct((tokens, QK), BF16)
    whole = jax.ShapeDtypeStruct((tokens, D), BF16)
    wtx, wop, wf, nbuf, lq, rk, vk, probs, ctx, emb, attn = pl.pallas_call(
        partial(attend_kernel, ring, chunks),
        out_shape=(
            jax.ShapeDtypeStruct((D, D), BF16),
            jax.ShapeDtypeStruct((D, QK), BF16),
            jax.ShapeDtypeStruct((D, FFN) if ring else (16, 128), BF16),
            jax.ShapeDtypeStruct((devices,) + pnorm.shape if ring else (1, 8, 128), F32),
            wide,
            wide,
            wide,
            jax.ShapeDtypeStruct((chunks, HEADS, SEQ, SEQ), BF16),
            wide,
            whole,
            own,
        ),
        in_specs=[vmem()] * 7,
        out_specs=(vmem(),) * 11,
        scratch_shapes=[pltpu.VMEM((D, ATT), BF16), pltpu.VMEM((HALF, SEQ), F32)]
        + sum_scratch(chunks, 1)
        + [dma(3, max(ring, 1))] * 4
        + [dma(2, chunks)] * 4,
        compiler_params=params(0),
    )(hidden_in, cols, keyrow, box_lanes(), packa, packf, pnorm)
    if ring:
        norm_full = nbuf[:, :4, :share].transpose(1, 0, 2).reshape(4, D)
    else:
        wf = wf_full
    norm_full = jnp.pad(norm_full, ((0, 4), (0, 0)))
    grad = jax.ShapeDtypeStruct((D, D), F32)
    mixed, gtwo, xone, rone, tback, gup, gdown, ntwo = pl.pallas_call(
        partial(forward_kernel, chunks),
        out_shape=(
            whole,
            own,
            own,
            jax.ShapeDtypeStruct((chunks, HALF, 128), F32),
            own,
            grad,
            grad,
            jax.ShapeDtypeStruct((16, D), F32),
        ),
        in_specs=[vmem()] * 5,
        out_specs=(pl.BlockSpec(memory_space=pl.ANY),) + (vmem(),) * 7,
        scratch_shapes=[pltpu.VMEM((tokens, D), BF16)] * 4
        + [pltpu.VMEM((HALF, D), F32), pltpu.VMEM((chunks, HALF, D), BF16)]
        + sum_scratch(chunks, 2)
        + [dma(chunks)] * 7
        + [dma(2, chunks)] * 4,
        compiler_params=params(1),
    )(attn, hidden_in, out_grad, norm_full, wf)
    count = max(ring, 1)
    buffers = []
    for width in (D, D, ATT):
        buffers += [pltpu.VMEM((count, share, width) if ring else (16, 128), BF16)] * 4
    small = (share, D) if ring else (16, 128)
    input_grad, reda, redup, reddown, nred = pl.pallas_call(
        partial(backward_kernel, ring, chunks),
        out_shape=(
            jax.ShapeDtypeStruct((tokens, D), F32),
            jax.ShapeDtypeStruct((share, ATT) if ring else (D, ATT), F32),
            jax.ShapeDtypeStruct(small, F32),
            jax.ShapeDtypeStruct(small, F32),
            jax.ShapeDtypeStruct((8, D), F32),
        ),
        in_specs=[vmem()] * 17,
        out_specs=(pl.BlockSpec(memory_space=pl.ANY),) + (vmem(),) * 4,
        scratch_shapes=[
            pltpu.VMEM((tokens, D), BF16),
            pltpu.VMEM((chunks, HALF, D), F32),
            pltpu.VMEM((tokens, D), BF16),
            pltpu.VMEM((tokens, QK), BF16),
            pltpu.VMEM((SEQ, SEQ), BF16),
            pltpu.VMEM((SEQ, QK), BF16),
            pltpu.VMEM((SEQ, SEQ), F32),
            pltpu.VMEM((D, ATT), F32),
            pltpu.VMEM((chunks, HALF, D), F32),
        ]
        + sum_scratch(chunks, 1)
        + [pltpu.VMEM((32, D), F32), pltpu.VMEM((count + 1, 8, D), F32)]
        + buffers
        + [dma(chunks)] * 5
        + [dma(2, chunks)] * 4
        + [dma(count + 1)] * 2
        + [dma(3, count)] * 4,
        compiler_params=params(2),
    )(
        tback,
        gtwo,
        xone,
        rone,
        norm_full,
        lq,
        rk,
        vk,
        probs,
        ctx,
        hidden_in,
        emb,
        wtx,
        wop,
        gup,
        gdown,
        ntwo,
    )
    position = lax.axis_index("dp")
    if not ring:
        reda, redup, reddown = (
            lax.psum_scatter(part, "dp", scatter_dimension=0, tiled=True)
            for part in (reda, gup, gdown)
        )
        nred = lax.psum(nred, ("dp", "mp")) * 0.5
    grad_norm = lax.dynamic_slice_in_dim(nred[:4], position * share, share, 1)
    grad_q, grad_k = split_pair(reda[:, :QK])
    grad_o, grad_v = split_pair(reda[:, QK : 2 * QK])
    grad_kb, grad_qb = split_pair(reda[:, 2 * QK :])
    grad_in = jnp.stack([grad_q, grad_k, grad_v, grad_qb, grad_kb])
    new_in = adam_step(
        attn_in, grad_in, attn_in_moment, attn_in_second, rate_matrix, decay_matrix
    )
    new_out = adam_step(
        attn_out, grad_o.T, attn_out_moment, attn_out_second, rate_matrix, decay_matrix
    )
    new_up = adam_step(ffn_in, redup, ffn_in_moment, ffn_in_second, rate_matrix, decay_matrix)
    new_down = adam_step(
        ffn_out, reddown.T, ffn_out_moment, ffn_out_second, rate_matrix, decay_matrix
    )
    new_norm = adam_step(norm_weight, grad_norm, norm_moment, norm_second, rate_norm, 0.0)
    return (mixed, input_grad) + new_in + new_out + new_up + new_down + new_norm


def solution(mesh):
    rows = P("dp", None)
    into = P(None, "dp", "mp")
    out = P("mp", "dp")
    up = P("dp", "mp")
    norm = P(None, "dp")
    return jax.shard_map(
        partial(per_device, mesh.shape["dp"]),
        mesh=mesh,
        in_specs=(rows, P("dp"), P("dp"), rows, rows)
        + (into,) * 3
        + (out,) * 3
        + (up,) * 3
        + (out,) * 3
        + (norm,) * 3,
        out_specs=(rows, rows) + (into,) * 3 + (out,) * 3 + (up,) * 3 + (out,) * 3 + (norm,) * 3,
        check_vma=False,
    )
```

time: 869 us -> 319 us (0.37); the launches traced: 857 us -> 318 us
  waiting for transfers between devices: 477 us -> 0 us
  Pallas kernels: 0 us -> 285 us
  blocking collectives: 98.8 us -> 0 us
  matrix products: 91.3 us -> 0 us
  local copies, waits for them, and re-layouts: 101 us -> 20.5 us
  other arithmetic: 72.2 us -> 12.2 us
  between operations: 15.3 us -> 1.02 us
    psum x5 -> x0, waiting for transfers between devices: 396 us -> none  [the longest x1 267 us: per_device(): summed = lax.psum((grad_in, grad_out, grad_up, grad_down, grad_norm), 'dp')]
    pallas_call x0 -> x3, Pallas kernels: none -> 285 us  [the longest x1 113 us: per_device(): pl.pallas_call(partial(attend_kernel, ring, chunks), out_shape=(jax.Shape...]
    dot_general x34 -> x0, matrix products: 88.1 us -> none  [the longest x1 15.5 us: per_device(): pre_active = jnp.dot(shared, weight_up, preferred_element_type=jnp.float32)]
    all_gather x3 -> x0, waiting for transfers between devices: 81 us -> none  [the longest x1 39.7 us: per_device(): lax.all_gather(ffn_in.astype(jnp.bfloat16), 'dp', axis=0, tiled=True)]
    all_gather x2 -> x0, blocking collectives: 61.7 us -> none  [the longest x1 35.6 us: per_device(): lax.all_gather(attn_out.astype(jnp.bfloat16), 'dp', axis=1, tiled=True)]
    psum x1 -> x0, blocking collectives: 37.1 us -> none  [per_device(): summed = lax.psum((grad_in, grad_out, grad_up, grad_down, grad_norm), 'dp')]
    reduce_sum x11 -> x0, other arithmetic: 28.2 us -> none  [the longest x2 9.84 us: layer_norm(): return shifted * lax.rsqrt(spread + epsilon_norm) * scaling + offset]
    another operation x17 -> x7, local copies, waits for them, and re-layouts: 23.9 us -> 2.55 us  [the longest x4 1.35 us: box_lanes(): jnp.stack([jnp.concatenate([frequency] * 4), jnp.concatenate([zero, zero,...]
  transfers between devices with their start and end apart: 8 -> 0, of which waited for: 8 -> 0; matrix products, arithmetic and copies ran while one was open for 8% -> 0% of each run, Pallas kernels for 0% -> 0%
where the time goes in v1:
time: 319 us; the launch traced here: 318 us
  Pallas kernels  285 us (89%)
  local copies, waits for them, and re-layouts  20.5 us (6%)
  other arithmetic  12.2 us (4%)
    pallas_call x1, Pallas kernels, per_device(): pl.pallas_call(partial(attend_kernel, ring, chunks), out_shape=(jax.Shape...  113 us
    pallas_call x1, Pallas kernels, per_device(): pl.pallas_call(partial(backward_kernel, ring, chunks), out_shape=(jax.Sha...  101 us
    pallas_call x1, Pallas kernels, per_device(): pl.pallas_call(partial(forward_kernel, chunks), out_shape=(whole, own, ow...  70.8 us
    unnamed x40, local copies, waits for them, and re-layouts  12.7 us
    sub x5, other arithmetic, adam_step(): weight - rate * (moment_hat / (jnp.sqrt(second_hat) + epsilon_adam) + dec...  8.16 us

profile of v1, /device:TPU:0, one launch (start us, length us, event | category | flops | bytes accessed | tf_op | source)
XLA Modules:
  0.0 318.2 jit_solution(155627638070932913)
XLA Ops:
  0.7 0.7 convert_element_type.44
  1.4 0.8 slice_convert_fusion.1
  2.2 1.2 copy.75.cols
  3.4 0.8 compare_select_fusion
  4.9 1.3 stack.24.lanes
  6.2 1.3 copy.68
  8.1 0.7 pad_maximum_fusion.1.packa
  8.9 0.7 pad_maximum_fusion.packf
  10.2 112.9 %shard_map.323 = (bf16[768,768]{1,0:T(8,128)(2,1)}, bf16[768,384]{1,0:T(8,128)(2,1)}, bf16[768,1536]{1,0:T(8,128)(2,1)}, f32[8,8,128]{2,1,0:T(8,128)}, bf16[1536...) custom-call(bf16[1536,768]{1,0:T(8,128)(2,1)} %hidden.5, ...), custom_call_target="tpu_custom_call" | custom-call | tf_op jit(solution)/shard_map/pallas_call | solution.py:912
  123.1 0.8 slice_bitcast_fusion
  124.6 70.8 %shard_map.324 = (bf16[1536,768]{1,0:T(8,128)(2,1)}, f32[3,256,768]{2,1,0:T(8,128)}, f32[3,256,768]{2,1,0:T(8,128)}, f32[3,256,128]{2,1,0:T(8,128)}, f32[3,256,7...) custom-call(f32[3,256,768]{2,1,0:T(8,128)} %get-tuple-element.41.attn, ...), custom_call_target="tpu_custom_call" | custom-call | tf_op jit(solution)/shard_map/pallas_call | solution.py:941
  195.4 100.8 %shard_map.325 = (f32[1536,768]{1,0:T(8,128)}, f32[96,1152]{1,0:T(8,128)}, f32[96,768]{1,0:T(8,128)}, f32[96,768]{1,0:T(8,128)}, f32[8,768]{1,0:T(8,128)}) custom-call(f32[3,256,768]{2,1,0:T(8,128)} %get-tuple-element.45.tback, f32[3,256,768]{2,1,0:T(8,128)} %get-tuple-element.46.gtwo, f32[3,256,768]{2,1,0:T(8,128)} %get-tuple-element.47.xone, ...), custom_call_target="tpu_custom_call" | custom-call | tf_op jit(solution)/shard_map/pallas_call | solution.py:967
  296.3 1.1 fusion.14
  299.4 1.2 copy.81
  300.7 1.4 multiply_subtract_fusion
  302.1 1.0 copy.84
  303.1 1.0 copy.85
  304.2 1.0 copy.86
  305.2 1.8 multiply_subtract_fusion.3
  307.0 2.1 multiply_subtract_fusion.2
  309.1 2.2 multiply_subtract_fusion.1
  311.3 0.7 multiply_subtract_fusion.4
  312.0 1.4 copy.93
  313.4 4.8 %copy.94 = f32[1536,768]{1,0:T(8,128)} copy(f32[1536,768]{1,0:T(8,128)} %get-tuple-element.148) | data formatting | bytes 9437184
  (67 shorter events, 4.5 us)
Async XLA Ops:
  0.7 7.1 %copy-start.5 = (f32[192,96]{1,0:T(8,128)S(1)}, f32[192,96]{1,0:T(8,128)}, u32[]{:S(2)}) copy-start(f32[192,96]{1,0:T(8,128)} %param.28) | copy-start | bytes 221188
  3.4 5.4 %copy-start.2 = (f32[768,96]{0,1:T(8,128)S(1)}, f32[768,96]{0,1:T(8,128)}, u32[]{:S(2)}) copy-start(f32[768,96]{0,1:T(8,128)} %param.34) | copy-start | bytes 884740
  6.2 2.6 copy-start.1
  7.5 2.1 copy-start.10
  296.3 2.3 copy-start.4
  298.6 0.8 copy-start.3
  302.1 3.1 copy-start.6
  302.1 3.1 copy-start.7
  302.1 3.0 copy-start.9
  302.1 4.9 %copy-start.8 = (f32[96,768]{1,0:T(8,128)S(1)}, f32[96,768]{1,0:T(8,128)}, u32[]{:S(2)}) copy-start(f32[96,768]{1,0:T(8,128)} %param.32) | copy-start | bytes 884740
  305.2 6.1 %copy-start.11 = (f32[8,768]{1,0:T(8,128)S(1)}, f32[8,768]{1,0:T(8,128)}, u32[]{:S(2)}) copy-start(f32[8,768]{1,0:T(8,128)} %get-tuple-element.64) | copy-start | bytes 73732
  305.2 6.1 %copy-start.12 = (f32[4,96]{1,0:T(4,128)S(1)}, f32[4,96]{1,0:T(4,128)}, u32[]{:S(2)}) copy-start(f32[4,96]{1,0:T(4,128)} %param.38) | copy-start | bytes 4612
  305.2 6.1 %copy-start.13 = (f32[4,96]{1,0:T(4,128)S(1)}, f32[4,96]{1,0:T(4,128)}, u32[]{:S(2)}) copy-start(f32[4,96]{1,0:T(4,128)} %param.39) | copy-start | bytes 4612
  305.2 6.8 %copy-start = (bf16[1536,768]{1,0:T(8,128)(2,1)S(1)}, bf16[1536,768]{1,0:T(8,128)(2,1)}, u32[]{:S(2)}) copy-start(bf16[1536,768]{1,0:T(8,128)(2,1)} %get-tuple-element.147) | copy-start | bytes 7077892

commit v2 on v1

v2 whole, which is shorter than its diff:
```python
from functools import partial
import math

import jax
import jax.numpy as jnp
from jax import lax
from jax.experimental import pallas as pl
from jax.experimental.pallas import tpu as pltpu
from jax.sharding import PartitionSpec as P

D = 768
HEAD_DIM = 64
SEQ = 512
HALF = SEQ // 2
STEP = 10
HEADS = 3
QK = HEADS * 128
ATT = 3 * QK
FFN = 2 * D

epsilon_norm = 1e-12
epsilon_adam = 1e-08
beta_first = 0.9
beta_second = 0.999
rate_matrix = 0.05
rate_norm = 0.2
decay_matrix = 0.01
masked_score = -1e30

F32 = jnp.float32
BF16 = jnp.bfloat16
VMEM_LIMIT = 60 * 1024 * 1024


def dot(a, b):
    return jnp.dot(a, b, preferred_element_type=F32)


def dot_nt(a, b):
    return lax.dot_general(a, b, (((1,), (1,)), ((), ())), preferred_element_type=F32)


def dot_tn(a, b):
    return lax.dot_general(a, b, (((0,), (0,)), ((), ())), preferred_element_type=F32)


def remote(src, dst, send, recv, device):
    return pltpu.make_async_remote_copy(
        src_ref=src,
        dst_ref=dst,
        send_sem=send,
        recv_sem=recv,
        device_id=device,
        device_id_type=pl.DeviceIdType.MESH,
    )


def steps(total, size, body):
    def run(i, carry):
        body(pl.multiple_of(i * size, size))
        return carry

    lax.fori_loop(0, total // size, run, 0)


def lower_half(shape):
    return lax.broadcasted_iota(jnp.int32, shape, len(shape) - 1) % 128 < HEAD_DIM


class Place:
    def __init__(self, ring):
        self.dp = lax.axis_index("dp")
        self.mp = lax.axis_index("mp")
        self.half = self.mp % 2
        self.pair = (self.dp, self.mp + 1 - 2 * self.half)
        self.across = (self.dp, (self.mp + 2) % 4)
        self.ring = ring
        self.z = self.dp // 2
        self.x = self.dp % 2
        self.xdev = (self.dp + 1 - 2 * self.x, self.mp)

    def zdev(self, k):
        return (((self.z + k) % self.ring) * 2 + self.x, self.mp)

    def came(self, k):
        return ((self.z + self.ring - k) % self.ring) * 2 + self.x

    def came_other(self, k):
        return ((self.z + self.ring - k) % self.ring) * 2 + 1 - self.x

    def greet(self):
        peers = [self.pair, self.across]
        if self.ring:
            peers += [self.xdev] + [self.zdev(k) for k in range(1, self.ring)]
        barrier = pltpu.get_barrier_semaphore()
        for peer in peers:
            pl.semaphore_signal(
                barrier, inc=1, device_id=peer, device_id_type=pl.DeviceIdType.MESH
            )
        pl.semaphore_wait(barrier, len(peers))

    def own(self, r):
        return pl.ds(pl.multiple_of(r * SEQ + self.half * HALF, HALF), HALF)

    def other(self, r):
        return pl.ds(pl.multiple_of(r * SEQ + (1 - self.half) * HALF, HALF), HALF)


class Gather:
    def __init__(self, place, kind, src, at, sems):
        self.p, self.src, self.at = place, src, at
        zs, zr, xs, xr = sems
        self.zs, self.zr, self.xs, self.xr = (
            zs.at[kind],
            zr.at[kind],
            xs.at[kind],
            xr.at[kind],
        )

    def along(self, k):
        p = self.p
        return remote(self.src, self.at(p.dp), self.zs.at[k], self.zr.at[k], p.zdev(k))

    def onward(self, k):
        p = self.p
        src = self.src if isinstance(k, int) and k == 0 else self.at(p.came(k))
        return remote(src, self.at(p.came(k)), self.xs.at[k], self.xr.at[k], p.xdev)

    def start_along(self):
        for k in range(1, self.p.ring):
            self.along(k).start()

    def forward(self, k):
        p = self.p
        remote(
            self.src, self.at(p.came(k)), self.zs.at[k], self.zr.at[k], p.zdev(k)
        ).wait_recv()
        self.onward(k).start()

    def forward_all(self):
        for k in range(1, self.p.ring):
            self.forward(k)

    def finish(self):
        p = self.p
        for k in range(p.ring):
            remote(
                self.src, self.at(p.came_other(k)), self.xs.at[k], self.xr.at[k], p.xdev
            ).wait_recv()
        for k in range(1, p.ring):
            self.along(k).wait_send()
        for k in range(p.ring):
            self.onward(k).wait_send()


class Sum:
    def __init__(self, place, parity, psend, precv, sums, yrecv, sems):
        self.p = place
        self.psend, self.precv = psend, precv
        self.sums, self.yrecv = sums, yrecv.at[parity]
        ps, pr, ys, yr = sems
        self.ps, self.pr, self.ys, self.yr = (
            ps.at[parity],
            pr.at[parity],
            ys.at[parity],
            yr.at[parity],
        )

    def to_pair(self, r):
        return remote(
            self.psend.at[r], self.precv.at[r], self.ps.at[r], self.pr.at[r], self.p.pair
        )

    def over(self, r):
        return remote(
            self.sums.at[r], self.yrecv.at[r], self.ys.at[r], self.yr.at[r], self.p.across
        )

    def give(self, r, value):
        self.psend[r] = value.astype(BF16)
        self.to_pair(r).start()

    def keep(self, r, value):
        self.to_pair(r).wait_recv()
        self.sums[r] = (value + self.precv[r].astype(F32)).astype(BF16)
        self.over(r).start()

    def wait(self, r):
        self.over(r).wait_recv()

    def total(self, r, rows):
        return self.sums[r, rows, :].astype(F32) + self.yrecv[r, rows, :].astype(F32)

    def close(self, r):
        self.to_pair(r).wait_send()
        self.over(r).wait_send()


def rolled(value):
    return pltpu.roll(value.astype(F32), HEAD_DIM, 1)


def embed_rows(coords, lanes, out, row):
    rows = pl.ds(row, 64)
    here = coords[rows, :]
    across, upward = here[:, 0:1], here[:, 1:2]
    frequency, second, shift = lanes[0:1, :], lanes[1:2, :], lanes[2:3, :]
    angle = (across + (upward - across) * second) * frequency
    turns = jnp.round(angle * (2.0 / math.pi))
    rest = ((angle - turns * 1.5703125) - turns * 4.837512969970703125e-4) - turns * (
        7.54978995489188216e-8
    )
    square = rest * rest
    sine = rest + rest * square * (
        -1.6666654611e-1 + square * (8.3321608736e-3 + square * -1.9515295891e-4)
    )
    cosine = (
        1.0
        - 0.5 * square
        + square
        * square
        * (
            4.166664568298827e-2
            + square * (-1.388731625493765e-3 + square * 2.443315711809948e-5)
        )
    )
    quarter = (turns + shift).astype(jnp.int32)
    value = jnp.where((quarter & 1) == 1, cosine, sine)
    out[rows, :] = jnp.where((quarter & 2) == 2, -value, value).astype(BF16)


def norm_of(values):
    center = jnp.mean(values, axis=-1, keepdims=True)
    shifted = values - center
    spread = jnp.mean(shifted * shifted, axis=-1, keepdims=True)
    scale = lax.rsqrt(spread + epsilon_norm)
    return shifted * scale, scale


def norm_back(upstream, normal, scale):
    first = jnp.mean(upstream, axis=-1, keepdims=True)
    second = jnp.mean(upstream * normal, axis=-1, keepdims=True)
    return (upstream - first - normal * second) * scale


def fold(values):
    rows, width = values.shape
    return jnp.sum(values.reshape(rows // 8, 8, width), axis=0)


class Scatter:
    def __init__(self, place, share, src, width, xsend, xrecv, zsend, zrecv, sems):
        self.p, self.share, self.src, self.width = place, share, src, width
        self.xsend, self.xrecv, self.zsend, self.zrecv = xsend, xrecv, zsend, zrecv
        self.xs, self.xr, self.zs, self.zr = sems

    def rows(self, k, x):
        d = ((self.p.z + k) % self.p.ring) * 2 + x
        return pl.ds(pl.multiple_of(d * self.share, self.share), self.share)

    def xcopy(self, k):
        return remote(
            self.xsend.at[k, :, : self.width],
            self.xrecv.at[k],
            self.xs.at[k],
            self.xr.at[k],
            self.p.xdev,
        )

    def zcopy(self, k):
        return remote(
            self.zsend.at[k, :, : self.width],
            self.zrecv.at[k],
            self.zs.at[k],
            self.zr.at[k],
            self.p.zdev(k),
        )

    def start(self, k):
        value = self.src[self.rows(k, 1 - self.p.x), : self.width]
        self.xsend[k, :, : self.width] = value.astype(BF16)
        self.xcopy(k).start()

    def middle(self, k):
        self.xcopy(k).wait_recv()
        value = self.src[self.rows(k, self.p.x), : self.width] + self.xrecv[k].astype(F32)
        self.zsend[k, :, : self.width] = value.astype(BF16)
        self.zcopy(k).start()

    def own(self, out):
        self.xcopy(0).wait_recv()
        out[...] = self.src[self.rows(0, self.p.x), : self.width] + self.xrecv[0].astype(F32)

    def sent(self):
        for k in range(self.p.ring):
            self.xcopy(k).wait_send()
        for k in range(1, self.p.ring):
            self.zcopy(k).wait_send()

    def finish(self, out):
        value = out[...]
        for k in range(1, self.p.ring):
            self.zcopy(k).wait_recv()
            value = value + self.zrecv[k].astype(F32)
        out[...] = value


def layer_kernel(
    ring,
    chunks,
    hidden,
    cols,
    keyrow,
    lanes,
    packa,
    packf,
    pnorm,
    out_grad,
    mixed,
    igrad,
    outa,
    outf,
    nout,
    wa,
    wf,
    nbuf,
    norm,
    wtx,
    wop,
    lq,
    rk,
    vk,
    probs,
    ctx,
    emb,
    big,
    ograd,
    xone,
    rone,
    gtwo,
    shared,
    active,
    slope,
    low_two,
    stage,
    grads,
    nsum,
    nrecv,
    xsend,
    zsend,
    fxrecv,
    fzrecv,
    axrecv,
    azrecv,
    psend,
    precv,
    sums,
    yrecv,
    free,
    gather_zs,
    gather_zr,
    gather_xs,
    gather_xr,
    ps,
    pr,
    ys,
    yr,
    share_s,
    share_r,
    out_s,
    out_r,
    out_l,
    ol,
    ns,
    nr,
    sxs,
    sxr,
    szs,
    szr,
):
    p = Place(ring)
    tokens = hidden.shape[0]

    def ograd_copy(r):
        return pltpu.make_async_copy(out_grad.at[p.own(r), :], ograd.at[r], ol.at[r])

    for r in range(chunks):
        ograd_copy(r).start()
    p.greet()
    sums_sems = (ps, pr, ys, yr)
    sum_a, sum_b, sum_c, sum_d = (
        Sum(p, stage_number % 2, psend, precv, sums, yrecv, sums_sems)
        for stage_number in range(4)
    )
    if ring:
        share = packa.shape[0]
        gather_sems = (gather_zs, gather_zr, gather_xs, gather_xr)

        def rows_of(ref):
            return lambda d: ref.at[pl.ds(pl.multiple_of(d * share, share), share), :]

        gather_a = Gather(p, 0, packa, rows_of(wa), gather_sems)
        gather_f = Gather(p, 1, packf, rows_of(wf), gather_sems)
        gather_n = Gather(p, 2, pnorm, lambda d: nbuf.at[d], gather_sems)
        gather_a.start_along()
        gather_a.onward(0).start()
        mine = pl.ds(pl.multiple_of(p.dp * share, share), share)
        wa[mine, :] = packa[...]
        wf[mine, :] = packf[...]
        nbuf[p.dp] = pnorm[...]
    else:
        wa[...] = packa[...]
        wf[...] = packf[...]
        norm[...] = pnorm[...]
    steps(tokens, 64, partial(embed_rows, cols, lanes, emb))
    if ring:
        gather_a.forward_all()
        gather_f.start_along()
        gather_n.start_along()
        gather_a.finish()
        gather_f.onward(0).start()
        gather_n.onward(0).start()

    def build(row):
        rows = pl.ds(row, 256)
        low = lower_half((256, 128))
        wtx[rows, :QK] = wa[rows, :QK]
        for h in range(HEADS):
            qk_cols = slice(h * 128, (h + 1) * 128)
            ov_cols = slice(QK + h * 128, QK + (h + 1) * 128)
            ov = wa[rows, ov_cols].astype(F32)
            wtx[rows, ov_cols] = jnp.where(low, rolled(wa[rows, qk_cols]), ov).astype(BF16)
            wop[rows, qk_cols] = jnp.where(low, 0.0, rolled(ov)).astype(BF16)

    steps(D, 256, build)

    def project(row):
        rows = pl.ds(row, HALF)
        text = dot(hidden[rows, :], wtx[...])
        box = dot(emb[rows, :], wa[:, 2 * QK :])
        low = lower_half((HALF, QK))
        lq[rows, :] = jnp.where(low, text[:, :QK], box).astype(BF16)
        rk[rows, :] = jnp.where(low, box, text[:, :QK]).astype(BF16)
        vk[rows, :] = text[:, QK:].astype(BF16)

    steps(tokens, HALF, project)
    scores = big.at[:HALF, :SEQ]
    pre = big.at[:HALF, :]
    dprob = big.at[:, :SEQ]

    def attend(r, side):
        start = pl.multiple_of(side * HALF, HALF)
        q_rows = pl.ds(pl.multiple_of(r * SEQ + start, HALF), HALF)
        k_rows = pl.ds(pl.multiple_of(r * SEQ, SEQ), SEQ)
        low = lower_half((HALF, 128))
        pages = cols[q_rows, 2:3]
        here = lax.broadcasted_iota(jnp.int32, (HALF, SEQ), 0) + start
        there = lax.broadcasted_iota(jnp.int32, (HALF, SEQ), 1)
        allowed = (pages == keyrow[r]) | (here == there)
        for h in range(HEADS):
            tile = slice(h * 128, (h + 1) * 128)
            left = lq[q_rows, tile]
            both = jnp.concatenate([left, jnp.where(low, left, jnp.zeros_like(left))], axis=1)
            right = jnp.concatenate([rk[k_rows, tile], vk[k_rows, tile]], axis=1)
            scores[...] = dot_nt(both, right)
            value = jnp.where(allowed, scores[...] * HEAD_DIM**-0.5, masked_score)
            raised = jnp.exp(value - jnp.max(value, axis=-1, keepdims=True))
            value = raised / jnp.sum(raised, axis=-1, keepdims=True)
            probs[r, h, pl.ds(start, HALF), :] = value.astype(BF16)
            found = dot(probs[r, h, pl.ds(start, HALF), :], vk[k_rows, tile])
            ctx[q_rows, tile] = jnp.where(low, pltpu.roll(found, HEAD_DIM, 1), 0.0).astype(BF16)
        return dot_nt(ctx[q_rows, :], wa[:, QK : 2 * QK])

    spread = ring - 1 == chunks

    def stage_a(r, carry):
        sum_a.give(r, attend(r, 1 - p.half))
        sum_a.keep(r, attend(r, p.half))
        if spread:
            gather_f.forward(r + 1)
        return carry

    lax.fori_loop(0, chunks, stage_a, 0)
    if ring:
        if not spread:
            gather_f.forward_all()
        gather_n.forward_all()
        gather_n.finish()
        norm[...] = jnp.concatenate([nbuf[d, :, :share] for d in range(2 * ring)], axis=1)
        gather_f.finish()
    gain_one, bias_one = norm[0:1, :], norm[1:2, :]
    gain_two, bias_two = norm[2:3, :], norm[3:4, :]

    def pass_on(ref, number, rows, r):
        view = ref.at[rows, :]
        return remote(view, view, share_s.at[number, r], share_r.at[number, r], p.pair)

    def up_down(rows_at):
        rows = pl.ds(rows_at, HALF)
        pre[...] = dot(shared[rows, :], wf[:, :D])

        def gelu(row):
            here = pl.ds(row, 64)
            there = pl.ds(pl.multiple_of(rows_at + row, 64), 64)
            value = pre[here, :]
            below = 0.5 + 0.5 * lax.erf(value * math.sqrt(0.5))
            active[there, :] = (value * below).astype(BF16)
            density = jnp.exp(-0.5 * value * value) * (1.0 / math.sqrt(2.0 * math.pi))
            slope[there, :] = (below + value * density).astype(BF16)

        steps(HALF, 64, gelu)
        return dot_nt(active[rows, :], wf[:, D:])

    def own_at(r):
        return pl.multiple_of(r * SEQ + p.half * HALF, HALF)

    def other_at(r):
        return pl.multiple_of(r * SEQ + (1 - p.half) * HALF, HALF)

    def stage_b(r, carry):
        sum_a.wait(r)

        def part(row):
            rows = pl.ds(pl.multiple_of(own_at(r) + row, 128), 128)
            here = pl.ds(row, 128)
            normal, scale = norm_of(hidden[rows, :].astype(F32) + sum_a.total(r, here))
            xone[r, here, :] = normal
            rone[r, here, :] = jnp.broadcast_to(scale, (128, 128))
            shared[rows, :] = (normal * gain_one + bias_one).astype(BF16)

        steps(HALF, 128, part)
        pass_on(shared, 0, p.own(r), r).start()
        sum_a.close(r)
        pass_on(shared, 0, p.other(r), r).wait_recv()
        sum_b.give(r, up_down(other_at(r)))
        sum_b.keep(r, up_down(own_at(r)))
        return carry

    lax.fori_loop(0, chunks, stage_b, 0)
    nsum[...] = jnp.zeros_like(nsum)

    def mixed_here(r):
        return pltpu.make_async_copy(stage.at[r], mixed.at[p.own(r), :], out_l.at[0, r])

    def mixed_pair(rows, r):
        return remote(stage.at[r], mixed.at[rows, :], out_s.at[0, r], out_r.at[0, r], p.pair)

    def back(rows_at):
        rows = pl.ds(rows_at, HALF)
        pre[...] = dot(low_two[rows, :], wf[:, D:])

        def times(row):
            here = pl.ds(row, 64)
            there = pl.ds(pl.multiple_of(rows_at + row, 64), 64)
            slope[there, :] = (pre[here, :] * slope[there, :].astype(F32)).astype(BF16)

        steps(HALF, 64, times)
        return dot_nt(slope[rows, :], wf[:, :D])

    def stage_c(r, carry):
        ograd_copy(r).wait()
        sum_b.wait(r)

        def part(row):
            rows = pl.ds(pl.multiple_of(own_at(r) + row, 128), 128)
            here = pl.ds(row, 128)
            residual = xone[r, here, :] * gain_one + bias_one + sum_b.total(r, here)
            normal, scale = norm_of(residual)
            stage[r, here, :] = (normal * gain_two + bias_two).astype(BF16)
            grad = ograd[r, here, :].astype(F32)
            value = norm_back(grad * gain_two, normal, scale)
            gtwo[r, here, :] = value
            low_two[rows, :] = value.astype(BF16)
            nsum[16:24, :] += fold(grad * normal)
            nsum[24:32, :] += fold(grad)

        steps(HALF, 128, part)
        pass_on(low_two, 1, p.own(r), r).start()
        mixed_here(r).start()
        mixed_pair(p.own(r), r).start()
        sum_b.close(r)
        pass_on(low_two, 1, p.other(r), r).wait_recv()
        sum_c.give(r, back(other_at(r)))
        sum_c.keep(r, back(own_at(r)))
        return carry

    lax.fori_loop(0, chunks, stage_c, 0)
    if ring:
        scatter_sems = (sxs, sxr, szs, szr)
        scatter_f = Scatter(
            p, share, grads, FFN, xsend, fxrecv, zsend, fzrecv, [s.at[0] for s in scatter_sems]
        )
        scatter_a = Scatter(
            p, share, grads, ATT, xsend, axrecv, zsend, azrecv, [s.at[1] for s in scatter_sems]
        )
    block = 4 * share if ring else D // 2

    def weight_blocks(work, scatter):
        def run(i, carry):
            place = (p.z // 2 + 1 + i) % (ring // 2) if ring else i
            work(pl.ds(pl.multiple_of(place * block, block), block))
            if ring:
                far = 1 - p.z % 2
                for line in (far, 1 - far):
                    scatter.start((2 * place + line + ring - p.z) % ring)
            return carry

        lax.fori_loop(0, D // block, run, 0)

    def ffn_weights(rows):
        grads[rows, :D] = grad_of(shared, rows, slope)
        grads[rows, D:] = grad_of(low_two, rows, active)

    def grad_of(left, rows, right):
        return dot_tn(left[:, rows], right[...])

    weight_blocks(ffn_weights, scatter_f if ring else None)

    def settle(r, carry):
        pass_on(shared, 0, p.own(r), r).wait_send()
        pass_on(low_two, 1, p.own(r), r).wait_send()
        return carry

    lax.fori_loop(0, chunks, settle, 0)
    pl.semaphore_signal(free, inc=1, device_id=p.pair, device_id_type=pl.DeviceIdType.MESH)
    if not ring:
        pltpu.sync_copy(grads, outf)
    low_one, gtext, gbox = shared, active, slope.at[:, :QK]
    gctx, gscore = slope.at[:SEQ, QK:], low_two.at[:SEQ, :SEQ]
    score_scale = HEAD_DIM**-0.5

    def attend_back(r):
        k_rows = pl.ds(pl.multiple_of(r * SEQ, SEQ), SEQ)
        for side in range(2):
            rows = pl.ds(pl.multiple_of(r * SEQ + side * HALF, HALF), HALF)
            gctx[side * HALF : (side + 1) * HALF, :] = dot(low_one[rows, :], wop[...]).astype(BF16)
        low = lower_half((SEQ, 128))
        for h in range(HEADS):
            tile = slice(h * 128, (h + 1) * 128)
            dprob[...] = dot_nt(gctx[:, tile], vk[k_rows, tile])

            def soften(row):
                rows = pl.ds(row, 256)
                grad = dprob[rows, :]
                prob = probs[r, h, rows, :].astype(F32)
                weighted = jnp.sum(prob * grad, axis=-1, keepdims=True)
                gscore[rows, :] = (prob * (grad - weighted)).astype(BF16)

            steps(SEQ, 256, soften)
            left = dot(gscore[...], rk[k_rows, tile]) * score_scale
            right = dot_tn(gscore[...], lq[k_rows, tile]) * score_scale
            value = dot_tn(probs[r, h], gctx[:, tile])
            gtext[k_rows, tile] = jnp.where(
                low, left + pltpu.roll(left, HEAD_DIM, 1), right + pltpu.roll(right, HEAD_DIM, 1)
            ).astype(BF16)
            gbox[k_rows, tile] = jnp.where(low, right, left).astype(BF16)
            gtext[k_rows, QK + h * 128 : QK + (h + 1) * 128] = value.astype(BF16)

    def partial_of(rows):
        return dot_nt(gtext[rows, :], wtx[...])

    pl.semaphore_wait(free, 1)

    def stage_d(r, carry):
        sum_c.wait(r)

        def part(row):
            rows = pl.ds(pl.multiple_of(own_at(r) + row, 128), 128)
            here = pl.ds(row, 128)
            grad = gtwo[r, here, :] + sum_c.total(r, here)
            normal = xone[r, here, :]
            value = norm_back(grad * gain_one, normal, rone[r, here, 0:1])
            gtwo[r, here, :] = value
            low_one[rows, :] = value.astype(BF16)
            nsum[0:8, :] += fold(grad * normal)
            nsum[8:16, :] += fold(grad)

        steps(HALF, 128, part)
        pass_on(low_one, 2, p.own(r), r).start()
        sum_c.close(r)
        pass_on(low_one, 2, p.other(r), r).wait_recv()
        attend_back(r)
        sum_d.give(r, partial_of(p.other(r)))
        sum_d.keep(r, partial_of(p.own(r)))
        if spread:
            scatter_f.middle(r + 1)
        return carry

    lax.fori_loop(0, chunks, stage_d, 0)
    if ring:
        if not spread:
            for k in range(1, ring):
                scatter_f.middle(k)
        scatter_f.own(outf)
        scatter_f.sent()

    def attention_weights(rows):
        text = grad_of(hidden, rows, gtext)
        grads[rows, :QK] = text[:, :QK]
        grads[rows, QK : 2 * QK] = text[:, QK:] + grad_of(low_one, rows, ctx)
        grads[rows, 2 * QK : ATT] = grad_of(emb, rows, gbox)

    weight_blocks(attention_weights, scatter_a if ring else None)
    for row in range(4):
        nsum[row : row + 1, :] = jnp.sum(nsum[row * 8 : row * 8 + 8, :], axis=0, keepdims=True)
    if ring:
        norm_pair = remote(nsum.at[0:8], nrecv.at[0], ns.at[0], nr.at[0], p.pair)
        norm_pair.start()
        scatter_a.middle(1)
        norm_pair.wait_recv()
        nsum[8:16, :] = nsum[0:8, :] + nrecv[0]
        norm_x = remote(nsum.at[8:16], nrecv.at[1], ns.at[1], nr.at[1], p.xdev)
        norm_x.start()
        for k in range(2, ring):
            scatter_a.middle(k)
        scatter_a.own(outa)
        norm_x.wait_recv()
        nsum[16:24, :] = nsum[8:16, :] + nrecv[1]
        norm_z = [
            remote(nsum.at[16:24], nrecv.at[1 + k], ns.at[1 + k], nr.at[1 + k], p.zdev(k))
            for k in range(1, ring)
        ]
        for copy in norm_z:
            copy.start()
    else:
        pltpu.sync_copy(grads.at[:, :ATT], outa)
        nout[...] = nsum[0:8, :]

    def igrad_here(r):
        return pltpu.make_async_copy(gtwo.at[r], igrad.at[p.own(r), :], out_l.at[1, r])

    def igrad_pair(rows, r):
        return remote(gtwo.at[r], igrad.at[rows, :], out_s.at[1, r], out_r.at[1, r], p.pair)

    def stage_e(r, carry):
        sum_d.wait(r)
        gtwo[r] = gtwo[r] + sum_d.total(r, slice(None))
        igrad_here(r).start()
        igrad_pair(p.own(r), r).start()
        sum_d.close(r)
        pass_on(low_one, 2, p.own(r), r).wait_send()
        mixed_here(r).wait()
        mixed_pair(p.own(r), r).wait_send()
        mixed_pair(p.other(r), r).wait_recv()
        return carry

    lax.fori_loop(0, chunks, stage_e, 0)
    if ring:
        scatter_f.finish(outf)
        scatter_a.finish(outa)
        scatter_a.sent()
        summed = nsum[16:24, :]
        for k in range(1, ring):
            norm_z[k - 1].wait_recv()
            summed = summed + nrecv[1 + k]
        nout[...] = summed
        for copy in [norm_pair, norm_x] + norm_z:
            copy.wait_send()

    def end(r, carry):
        igrad_here(r).wait()
        igrad_pair(p.own(r), r).wait_send()
        igrad_pair(p.other(r), r).wait_recv()
        return carry

    lax.fori_loop(0, chunks, end, 0)


def adam_step(weight, gradient, moment, second, rate, decay):
    moment_new = beta_first * moment + (1.0 - beta_first) * gradient
    second_new = beta_second * second + (1.0 - beta_second) * gradient * gradient
    moment_hat = moment_new / (1.0 - beta_first**STEP)
    second_hat = second_new / (1.0 - beta_second**STEP)
    weight_new = weight - rate * (
        moment_hat / (jnp.sqrt(second_hat) + epsilon_adam) + decay * weight
    )
    return (weight_new, moment_new, second_new)


def vmem():
    return pl.BlockSpec(memory_space=pltpu.VMEM)


def dma(*shape):
    return pltpu.SemaphoreType.DMA(shape)


def interleave(first, second):
    rows = first.shape[0]
    pair = [part.reshape(rows, HEADS, 1, HEAD_DIM) for part in (first, second)]
    return jnp.concatenate(pair, axis=2).reshape(rows, QK)


def split_pair(both):
    rows = both.shape[0]
    pair = both.reshape(rows, HEADS, 2, HEAD_DIM)
    return pair[:, :, 0].reshape(rows, QK // 2), pair[:, :, 1].reshape(rows, QK // 2)


def box_lanes():
    quarter = D // 4
    ladder = jnp.arange(quarter).astype(F32)
    frequency = jnp.exp(ladder * (-math.log(10000.0) / quarter))
    zero, one = jnp.zeros((quarter,), F32), jnp.ones((quarter,), F32)
    return jnp.stack(
        [
            jnp.concatenate([frequency] * 4),
            jnp.concatenate([zero, zero, one, one]),
            jnp.concatenate([zero, one, zero, one]),
        ]
        + [jnp.zeros((D,), F32)] * 5
    )


def per_device(
    devices,
    hidden_in,
    page_ids,
    pad_mask,
    boxes,
    out_grad,
    attn_in,
    attn_in_moment,
    attn_in_second,
    attn_out,
    attn_out_moment,
    attn_out_second,
    ffn_in,
    ffn_in_moment,
    ffn_in_second,
    ffn_out,
    ffn_out_moment,
    ffn_out_second,
    norm_weight,
    norm_moment,
    norm_second,
):
    tokens = hidden_in.shape[0]
    chunks = tokens // SEQ
    share = attn_in.shape[1]
    ring = devices // 2 if devices % 4 == 0 and share % 32 == 0 else 0
    low_in = attn_in.astype(BF16)
    packa = jnp.concatenate(
        [
            interleave(low_in[0], low_in[1]),
            interleave(attn_out.T.astype(BF16), low_in[2]),
            interleave(low_in[4], low_in[3]),
        ],
        axis=1,
    )
    packf = jnp.concatenate([ffn_in.astype(BF16), ffn_out.T.astype(BF16)], axis=1)
    pnorm = jnp.pad(norm_weight, ((0, 4), (0, -share % 128)))
    if not ring:
        packa = lax.all_gather(packa, "dp", axis=0, tiled=True)
        packf = lax.all_gather(packf, "dp", axis=0, tiled=True)
        pnorm = lax.all_gather(norm_weight, "dp", axis=1, tiled=True)
        pnorm = jnp.pad(pnorm, ((0, 4), (0, 0)))
    pages = page_ids.astype(F32)
    cols = jnp.stack([boxes[:, 0].astype(F32), boxes[:, 1].astype(F32), pages], axis=1)
    keyrow = jnp.where(pad_mask == 0, pages, -1.0).reshape(chunks, 1, SEQ)
    count = max(ring, 1)
    any_space = pl.BlockSpec(memory_space=pl.ANY)
    inner = share if ring else 16
    tile = pltpu.VMEM((tokens, D), BF16)
    wide = pltpu.VMEM((tokens, QK), BF16)
    own = pltpu.VMEM((chunks, HALF, D), F32)
    own_low = pltpu.VMEM((chunks, HALF, D), BF16)
    att_share = pltpu.VMEM((count, inner, ATT), BF16)
    ffn_share = pltpu.VMEM((count, inner, FFN), BF16)
    mixed, input_grad, reda, redf, nred = pl.pallas_call(
        partial(layer_kernel, ring, chunks),
        out_shape=(
            jax.ShapeDtypeStruct((tokens, D), BF16),
            jax.ShapeDtypeStruct((tokens, D), F32),
            jax.ShapeDtypeStruct((share if ring else D, ATT), F32),
            jax.ShapeDtypeStruct((share if ring else D, FFN), F32),
            jax.ShapeDtypeStruct((8, D), F32),
        ),
        in_specs=[vmem()] * 7 + [any_space],
        out_specs=(any_space,) * 2 + (vmem() if ring else any_space,) * 2 + (vmem(),),
        scratch_shapes=[
            pltpu.VMEM((D, ATT), BF16),
            pltpu.VMEM((D, FFN), BF16),
            pltpu.VMEM((2 * count,) + pnorm.shape, F32),
            pltpu.VMEM((8, D), F32),
            pltpu.VMEM((D, D), BF16),
            pltpu.VMEM((D, QK), BF16),
            wide,
            wide,
            wide,
            pltpu.VMEM((chunks, HEADS, SEQ, SEQ), BF16),
            wide,
            tile,
            pltpu.VMEM((SEQ, D), F32),
            own_low,
            own,
            pltpu.VMEM((chunks, HALF, 128), F32),
            own,
            tile,
            tile,
            tile,
            tile,
            own_low,
            pltpu.VMEM((D, FFN), F32),
            pltpu.VMEM((32, D), F32),
            pltpu.VMEM((count + 1, 8, D), F32),
            ffn_share,
            ffn_share,
            ffn_share,
            ffn_share,
            att_share,
            att_share,
            own_low,
            own_low,
            own_low,
            pltpu.VMEM((2, chunks, HALF, D), BF16),
            pltpu.SemaphoreType.REGULAR,
        ]
        + [dma(3, count)] * 4
        + [dma(2, chunks)] * 4
        + [dma(3, chunks)] * 2
        + [dma(2, chunks)] * 3
        + [dma(chunks)]
        + [dma(count + 1)] * 2
        + [dma(2, count)] * 4,
        compiler_params=pltpu.CompilerParams(
            collective_id=0, has_side_effects=True, vmem_limit_bytes=VMEM_LIMIT
        ),
    )(hidden_in, cols, keyrow, box_lanes(), packa, packf, pnorm, out_grad)
    redup, reddown = redf[:, :D], redf[:, D:]
    position = lax.axis_index("dp")
    if not ring:
        reda, redup, reddown = (
            lax.psum_scatter(part, "dp", scatter_dimension=0, tiled=True)
            for part in (reda, redup, reddown)
        )
        nred = lax.psum(nred, ("dp", "mp")) * 0.5
    grad_norm = lax.dynamic_slice_in_dim(nred[:4], position * share, share, 1)
    grad_q, grad_k = split_pair(reda[:, :QK])
    grad_o, grad_v = split_pair(reda[:, QK : 2 * QK])
    grad_kb, grad_qb = split_pair(reda[:, 2 * QK :])
    grad_in = jnp.stack([grad_q, grad_k, grad_v, grad_qb, grad_kb])
    new_in = adam_step(
        attn_in, grad_in, attn_in_moment, attn_in_second, rate_matrix, decay_matrix
    )
    new_out = adam_step(
        attn_out, grad_o.T, attn_out_moment, attn_out_second, rate_matrix, decay_matrix
    )
    new_up = adam_step(ffn_in, redup, ffn_in_moment, ffn_in_second, rate_matrix, decay_matrix)
    new_down = adam_step(
        ffn_out, reddown.T, ffn_out_moment, ffn_out_second, rate_matrix, decay_matrix
    )
    new_norm = adam_step(norm_weight, grad_norm, norm_moment, norm_second, rate_norm, 0.0)
    return (mixed, input_grad) + new_in + new_out + new_up + new_down + new_norm


def solution(mesh):
    rows = P("dp", None)
    into = P(None, "dp", "mp")
    out = P("mp", "dp")
    up = P("dp", "mp")
    norm = P(None, "dp")
    return jax.shard_map(
        partial(per_device, mesh.shape["dp"]),
        mesh=mesh,
        in_specs=(rows, P("dp"), P("dp"), rows, rows)
        + (into,) * 3
        + (out,) * 3
        + (up,) * 3
        + (out,) * 3
        + (norm,) * 3,
        out_specs=(rows, rows) + (into,) * 3 + (out,) * 3 + (up,) * 3 + (out,) * 3 + (norm,) * 3,
        check_vma=False,
    )
```

time: 319 us -> 218 us (0.68)
  Pallas kernels: 285 us -> 185 us
    pallas_call x3 -> x1, Pallas kernels: 285 us -> 185 us  [per_device(): pl.pallas_call(partial(layer_kernel, ring, chunks), out_shape=(jax.ShapeD...]
    unnamed x40 -> x34, local copies, waits for them, and re-layouts: 12.7 us -> 12.6 us
where the time goes in v2:
time: 218 us
  Pallas kernels  185 us (85%)
  local copies, waits for them, and re-layouts  19 us (9%)
  other arithmetic  12.2 us (6%)
    pallas_call x1, Pallas kernels, per_device(): pl.pallas_call(partial(layer_kernel, ring, chunks), out_shape=(jax.ShapeD...  185 us
    unnamed x34, local copies, waits for them, and re-layouts  12.6 us
    sub x5, other arithmetic, adam_step(): weight - rate * (moment_hat / (jnp.sqrt(second_hat) + epsilon_adam) + dec...  8.21 us

profile of v2, /device:TPU:0, one launch (start us, length us, event | category | flops | bytes accessed | tf_op | source)
XLA Modules:
  0.0 217.6 jit_solution(6713287223192389648)
XLA Ops:
  0.7 0.7 convert_element_type.42
  1.4 0.8 slice_convert_fusion.1
  2.2 1.2 copy.73.cols
  3.4 0.8 compare_select_fusion
  4.2 0.6 reshape.58.keyrow
  4.9 1.3 stack.24.lanes
  6.2 1.3 copy.66
  8.1 0.7 pad_maximum_fusion.1.packa
  8.9 0.7 pad_maximum_fusion.packf
  9.6 0.6 pad.4.pnorm
  10.2 185.5 %shard_map.323 = (bf16[1536,768]{1,0:T(8,128)(2,1)}, f32[1536,768]{1,0:T(8,128)}, f32[96,1152]{1,0:T(8,128)}, f32[96,1536]{1,0:T(8,128)}, f32[8,768]{1,0:T(8,128)}) custom-call(bf16[1536,768]{1,0:T(8,128)(2,1)} %hidden.1, f32[1536,3]{1,0:T(8,128)} %copy.73.cols, f32[3,1,512]{2,1,0:T(1,128)} %reshape.58.keyrow, f32[8,768]{1,0:T(8,128)} %stack.24.lanes, ...), custom_call_target="tpu_custom_call" | custom-call | tf_op jit(solution)/shard_map/pallas_call | solution.py:870
  195.7 1.1 fusion.14
  197.2 0.7 fusion.16
  198.8 1.2 copy.78
  200.1 1.4 multiply_subtract_fusion
  201.5 1.0 copy.81
  202.5 1.0 copy.82
  203.5 1.0 copy.83
  204.5 1.9 multiply_subtract_fusion.3
  206.5 2.1 multiply_subtract_fusion.2
  208.6 2.1 multiply_subtract_fusion.1
  210.7 0.7 multiply_subtract_fusion.4
  211.4 1.4 copy.90
  212.8 4.8 %copy.91 = f32[1536,768]{1,0:T(8,128)} copy(f32[1536,768]{1,0:T(8,128)} %get-tuple-element.110) | data formatting | bytes 9437184
  (55 shorter events, 1.9 us)
Async XLA Ops:
  0.7 7.1 %copy-start.6 = (f32[192,96]{1,0:T(8,128)S(1)}, f32[192,96]{1,0:T(8,128)}, u32[]{:S(2)}) copy-start(f32[192,96]{1,0:T(8,128)} %param.28) | copy-start | bytes 221188
  3.4 5.4 %copy-start.2 = (f32[768,96]{0,1:T(8,128)S(1)}, f32[768,96]{0,1:T(8,128)}, u32[]{:S(2)}) copy-start(f32[768,96]{0,1:T(8,128)} %param.34) | copy-start | bytes 884740
  6.2 2.6 %copy-start.1 = (f32[96,768]{1,0:T(8,128)S(1)}, f32[96,768]{1,0:T(8,128)}, u32[]{:S(2)}) copy-start(f32[96,768]{1,0:T(8,128)} %param.31) | copy-start | bytes 884740
  7.5 2.1 copy-start.7
  195.7 2.3 %copy-start.5 = (f32[5,96,192]{2,1,0:T(8,128)S(1)}, f32[5,96,192]{2,1,0:T(8,128)}, u32[]{:S(2)}) copy-start(f32[5,96,192]{2,1,0:T(8,128)} %param.26) | copy-start | bytes 1105924
  198.1 0.8 copy-start.3
  201.5 5.0 %copy-start.4 = (f32[96,1536]{1,0:T(8,128)S(1)}, f32[96,1536]{1,0:T(8,128)}, u32[]{:S(2)}) copy-start(f32[96,1536]{1,0:T(8,128)} %get-tuple-element.25) | copy-start | bytes 1769476
  204.5 6.1 %copy-start.8 = (f32[8,768]{1,0:T(8,128)S(1)}, f32[8,768]{1,0:T(8,128)}, u32[]{:S(2)}) copy-start(f32[8,768]{1,0:T(8,128)} %get-tuple-element.26) | copy-start | bytes 73732
  204.5 6.1 %copy-start.9 = (f32[4,96]{1,0:T(4,128)S(1)}, f32[4,96]{1,0:T(4,128)}, u32[]{:S(2)}) copy-start(f32[4,96]{1,0:T(4,128)} %param.38) | copy-start | bytes 4612
  204.5 6.1 %copy-start.10 = (f32[4,96]{1,0:T(4,128)S(1)}, f32[4,96]{1,0:T(4,128)}, u32[]{:S(2)}) copy-start(f32[4,96]{1,0:T(4,128)} %param.39) | copy-start | bytes 4612
  204.5 6.8 %copy-start = (bf16[1536,768]{1,0:T(8,128)(2,1)S(1)}, bf16[1536,768]{1,0:T(8,128)(2,1)}, u32[]{:S(2)}) copy-start(bf16[1536,768]{1,0:T(8,128)(2,1)} %get-tuple-element.109) | copy-start | bytes 7077892

commit v3 on v2

--- a/solution.py
+++ b/solution.py
@@ -3,6 +3,7 @@
 
 import jax
 import jax.numpy as jnp
+import numpy as np
 from jax import lax
 from jax.experimental import pallas as pl
 from jax.experimental.pallas import tpu as pltpu
@@ -82,12 +83,6 @@
     def zdev(self, k):
         return (((self.z + k) % self.ring) * 2 + self.x, self.mp)
 
-    def came(self, k):
-        return ((self.z + self.ring - k) % self.ring) * 2 + self.x
-
-    def came_other(self, k):
-        return ((self.z + self.ring - k) % self.ring) * 2 + 1 - self.x
-
     def greet(self):
         peers = [self.pair, self.across]
         if self.ring:
@@ -107,8 +102,8 @@
 
 
 class Gather:
-    def __init__(self, place, kind, src, at, sems):
-        self.p, self.src, self.at = place, src, at
+    def __init__(self, place, kind, at, sems):
+        self.p, self.at = place, at
         zs, zr, xs, xr = sems
         self.zs, self.zr, self.xs, self.xr = (
             zs.at[kind],
@@ -117,40 +112,61 @@
             xr.at[kind],
         )
 
-    def along(self, k):
+    def hop(self, line, up):
         p = self.p
-        return remote(self.src, self.at(p.dp), self.zs.at[k], self.zr.at[k], p.zdev(k))
-
-    def onward(self, k):
+        view = self.at(2 * line + p.x)
+        peer = (p.dp + 2, p.mp) if up else (p.dp - 2, p.mp)
+        return remote(view, view, self.zs.at[int(up), line], self.zr.at[line], peer)
+
+    def side(self, line, x):
+        view = self.at(2 * line + x)
+        return remote(view, view, self.xs.at[line], self.xr.at[line], self.p.xdev)
+
+    def send(self, line, up):
         p = self.p
-        src = self.src if isinstance(k, int) and k == 0 else self.at(p.came(k))
-        return remote(src, self.at(p.came(k)), self.xs.at[k], self.xr.at[k], p.xdev)
-
-    def start_along(self):
-        for k in range(1, self.p.ring):
-            self.along(k).start()
-
-    def forward(self, k):
+
+        @pl.when(p.z < p.ring - 1 if up else p.z > 0)
+        def _():
+            self.hop(line, up).start()
+
+    def start(self):
+        self.send(self.p.z, True)
+        self.send(self.p.z, False)
+
+    def cross(self):
+        self.side(self.p.z, self.p.x).start()
+
+    def step(self, s):
         p = self.p
-        remote(
-            self.src, self.at(p.came(k)), self.zs.at[k], self.zr.at[k], p.zdev(k)
-        ).wait_recv()
-        self.onward(k).start()
-
-    def forward_all(self):
-        for k in range(1, self.p.ring):
-            self.forward(k)
+
+        @pl.when(p.z >= s)
+        def _():
+            self.hop(p.z - s, True).wait_recv()
+            self.send(p.z - s, True)
+            self.side(p.z - s, p.x).start()
+
+        @pl.when(p.z + s < p.ring)
+        def _():
+            self.hop(p.z + s, False).wait_recv()
+            self.send(p.z + s, False)
+            self.side(p.z + s, p.x).start()
 
     def finish(self):
+        for line in range(self.p.ring):
+            self.side(line, 1 - self.p.x).wait_recv()
+
+    def drain(self):
         p = self.p
-        for k in range(p.ring):
-            remote(
-                self.src, self.at(p.came_other(k)), self.xs.at[k], self.xr.at[k], p.xdev
-            ).wait_recv()
-        for k in range(1, p.ring):
-            self.along(k).wait_send()
-        for k in range(p.ring):
-            self.onward(k).wait_send()
+        for line in range(p.ring):
+            self.side(line, p.x).wait_send()
+
+            @pl.when((p.z >= line) & (p.z < p.ring - 1))
+            def _():
+                self.hop(line, True).wait_send()
+
+            @pl.when((p.z <= line) & (p.z > 0))
+            def _():
+                self.hop(line, False).wait_send()
 
 
 class Sum:
@@ -308,13 +324,12 @@
 def layer_kernel(
     ring,
     chunks,
-    hidden,
-    cols,
-    keyrow,
+    hidden_hbm,
+    boxes,
+    pages,
+    padding,
     lanes,
-    packa,
-    packf,
-    pnorm,
+    weights,
     out_grad,
     mixed,
     igrad,
@@ -325,6 +340,9 @@
     wf,
     nbuf,
     norm,
+    tags,
+    cols,
+    hidden,
     wtx,
     wop,
     lq,
@@ -373,6 +391,7 @@
     ol,
     ns,
     nr,
+    hs,
     sxs,
     sxr,
     szs,
@@ -384,42 +403,67 @@
     def ograd_copy(r):
         return pltpu.make_async_copy(out_grad.at[p.own(r), :], ograd.at[r], ol.at[r])
 
+    hidden_copy = pltpu.make_async_copy(hidden_hbm, hidden, hs)
+    hidden_copy.start()
     for r in range(chunks):
         ograd_copy(r).start()
-    p.greet()
     sums_sems = (ps, pr, ys, yr)
     sum_a, sum_b, sum_c, sum_d = (
         Sum(p, stage_number % 2, psend, precv, sums, yrecv, sums_sems)
         for stage_number in range(4)
     )
     if ring:
-        share = packa.shape[0]
+        attn_in, attn_out, ffn_in, ffn_out, norm_in = weights
+        share = ffn_in.shape[0]
         gather_sems = (gather_zs, gather_zr, gather_xs, gather_xr)
 
         def rows_of(ref):
             return lambda d: ref.at[pl.ds(pl.multiple_of(d * share, share), share), :]
 
-        gather_a = Gather(p, 0, packa, rows_of(wa), gather_sems)
-        gather_f = Gather(p, 1, packf, rows_of(wf), gather_sems)
-        gather_n = Gather(p, 2, pnorm, lambda d: nbuf.at[d], gather_sems)
-        gather_a.start_along()
-        gather_a.onward(0).start()
+        gather_a = Gather(p, 0, rows_of(wa), gather_sems)
+        gather_f = Gather(p, 1, rows_of(wf), gather_sems)
+        gather_n = Gather(p, 2, lambda d: nbuf.at[d], gather_sems)
         mine = pl.ds(pl.multiple_of(p.dp * share, share), share)
-        wa[mine, :] = packa[...]
-        wf[mine, :] = packf[...]
-        nbuf[p.dp] = pnorm[...]
+        wa[mine, :] = pack_attention(attn_in, attn_out)
+        p.greet()
+        gather_a.start()
+        gather_a.cross()
+        wf[mine, :D] = ffn_in[...].astype(BF16)
+        wf[mine, D:] = ffn_out[...].astype(BF16)
+        nbuf[p.dp] = jnp.zeros_like(nbuf[0])
+        nbuf[p.dp, 0:4, :share] = norm_in[...]
     else:
-        wa[...] = packa[...]
-        wf[...] = packf[...]
-        norm[...] = pnorm[...]
-    steps(tokens, 64, partial(embed_rows, cols, lanes, emb))
+        p.greet()
+        wa[...], wf[...], norm[...] = (part[...] for part in weights)
+    key = jnp.where(padding[...] == 0, pages[...], -1)
+    tags[...] = jnp.zeros_like(tags)
+    tags[0:2, :] = boxes[...].astype(F32)
+    for row in range(tokens // 128):
+        span = slice(row * 128, row * 128 + 128)
+        tags[2:3, span] = pages[row : row + 1, :].astype(F32)
+        tags[3:4, span] = key[row : row + 1, :].astype(F32)
+    for row in range(0, tokens, SEQ):
+        cols[row : row + SEQ, 0:8] = tags[:, row : row + SEQ].T
+    parts = max(ring - 1, 1) if tokens % (64 * max(ring - 1, 1)) == 0 else 1
+    for part in range(parts):
+        base = part * (tokens // parts)
+        steps(
+            tokens // parts,
+            64,
+            lambda row: embed_rows(cols, lanes, emb, pl.multiple_of(base + row, 64)),
+        )
+        if ring and part + 1 < parts:
+            gather_a.step(part + 1)
     if ring:
-        gather_a.forward_all()
-        gather_f.start_along()
-        gather_n.start_along()
+        gather_f.start()
+        gather_n.start()
+        for s in range(parts, ring):
+            gather_a.step(s)
+        gather_f.cross()
+        gather_n.cross()
         gather_a.finish()
-        gather_f.onward(0).start()
-        gather_n.onward(0).start()
+        gather_f.step(1)
+        gather_n.step(1)
 
     def build(row):
         rows = pl.ds(row, 256)
@@ -433,6 +477,7 @@
             wop[rows, qk_cols] = jnp.where(low, 0.0, rolled(ov)).astype(BF16)
 
     steps(D, 256, build)
+    hidden_copy.wait()
 
     def project(row):
         rows = pl.ds(row, HALF)
@@ -444,6 +489,9 @@
         vk[rows, :] = text[:, QK:].astype(BF16)
 
     steps(tokens, HALF, project)
+    if ring > 2:
+        gather_f.step(2)
+        gather_n.step(2)
     scores = big.at[:HALF, :SEQ]
     pre = big.at[:HALF, :]
     dprob = big.at[:, :SEQ]
@@ -456,7 +504,7 @@
         pages = cols[q_rows, 2:3]
         here = lax.broadcasted_iota(jnp.int32, (HALF, SEQ), 0) + start
         there = lax.broadcasted_iota(jnp.int32, (HALF, SEQ), 1)
-        allowed = (pages == keyrow[r]) | (here == there)
+        allowed = (pages == tags[3:4, k_rows]) | (here == there)
         for h in range(HEADS):
             tile = slice(h * 128, (h + 1) * 128)
             left = lq[q_rows, tile]
@@ -476,15 +524,20 @@
     def stage_a(r, carry):
         sum_a.give(r, attend(r, 1 - p.half))
         sum_a.keep(r, attend(r, p.half))
-        if spread:
-            gather_f.forward(r + 1)
+        if ring > 3:
+
+            @pl.when(r == 0)
+            def _():
+                gather_f.step(3)
+                gather_n.step(3)
+
         return carry
 
     lax.fori_loop(0, chunks, stage_a, 0)
     if ring:
-        if not spread:
-            gather_f.forward_all()
-        gather_n.forward_all()
+        for s in range(4, ring):
+            gather_f.step(s)
+            gather_n.step(s)
         gather_n.finish()
         norm[...] = jnp.concatenate([nbuf[d, :, :share] for d in range(2 * ring)], axis=1)
         gather_f.finish()
@@ -746,6 +799,8 @@
 
     lax.fori_loop(0, chunks, stage_e, 0)
     if ring:
+        for gather in (gather_a, gather_f, gather_n):
+            gather.drain()
         scatter_f.finish(outf)
         scatter_a.finish(outa)
         scatter_a.sent()
@@ -753,7 +808,12 @@
         for k in range(1, ring):
             norm_z[k - 1].wait_recv()
             summed = summed + nrecv[1 + k]
-        nout[...] = summed
+        for d in range(2 * ring):
+
+            @pl.when(p.dp == d)
+            def _():
+                nout[:, :share] = summed[:, d * share : (d + 1) * share]
+
         for copy in [norm_pair, norm_x] + norm_z:
             copy.wait_send()
 
@@ -785,31 +845,96 @@
     return pltpu.SemaphoreType.DMA(shape)
 
 
+def heads_of(value):
+    return [value[:, h * HEAD_DIM : (h + 1) * HEAD_DIM] for h in range(value.shape[1] // HEAD_DIM)]
+
+
 def interleave(first, second):
-    rows = first.shape[0]
-    pair = [part.reshape(rows, HEADS, 1, HEAD_DIM) for part in (first, second)]
-    return jnp.concatenate(pair, axis=2).reshape(rows, QK)
+    pairs = zip(heads_of(first), heads_of(second))
+    return jnp.concatenate([part for pair in pairs for part in pair], axis=1)
 
 
 def split_pair(both):
-    rows = both.shape[0]
-    pair = both.reshape(rows, HEADS, 2, HEAD_DIM)
-    return pair[:, :, 0].reshape(rows, QK // 2), pair[:, :, 1].reshape(rows, QK // 2)
+    parts = heads_of(both)
+    return jnp.concatenate(parts[::2], axis=1), jnp.concatenate(parts[1::2], axis=1)
+
+
+def pack_attention(attn_in, attn_out):
+    low = [attn_in[i].astype(BF16) for i in range(5)]
+    return jnp.concatenate(
+        [
+            interleave(low[0], low[1]),
+            interleave(attn_out[...].T.astype(BF16), low[2]),
+            interleave(low[4], low[3]),
+        ],
+        axis=1,
+    )
+
+
+def finish_kernel(*refs):
+    grads, (mixed_in, igrad_in), olds = refs[:3], refs[3:5], refs[5:20]
+    (mixed, igrad), news, held, made = refs[20:22], refs[22:37], refs[37:55], refs[55:70]
+    passing, (in_sems, out_sems, fetch_sems, copy_sems) = refs[70:72], refs[72:]
+    reads = [
+        pltpu.make_async_copy(src, dst, in_sems.at[i])
+        for i, (src, dst) in enumerate(zip(grads + olds, held))
+    ]
+    fetches, copies = [], []
+    for src, mid, dst in zip((mixed_in, igrad_in), passing, (mixed, igrad)):
+        size = src.shape[0] // 4
+        for part in range(4):
+            rows, i = pl.ds(part * size, size), len(copies)
+            fetches.append(
+                pltpu.make_async_copy(src.at[rows, :], mid.at[rows, :], fetch_sems.at[i])
+            )
+            copies.append(
+                pltpu.make_async_copy(mid.at[rows, :], dst.at[rows, :], copy_sems.at[i])
+            )
+    for copy in reads + fetches:
+        copy.start()
+    writes = [
+        pltpu.make_async_copy(src, dst, out_sems.at[i])
+        for i, (src, dst) in enumerate(zip(made, news))
+    ]
+    for fetch, copy in zip(fetches, copies):
+        fetch.wait()
+        copy.start()
+    for copy in reads[:3]:
+        copy.wait()
+    reda, redf, nred = held[:3]
+    held = held[3:]
+
+    def update(number, gradients, rate, decay):
+        for copy in reads[3 + 3 * number : 6 + 3 * number]:
+            copy.wait()
+        for at, gradient in gradients:
+            old = [held[3 * number + i][at] for i in range(3)]
+            new = adam_step(old[0], gradient, old[1], old[2], rate, decay)
+            for i in range(3):
+                made[3 * number + i][at] = new[i]
+        for copy in writes[3 * number : 3 * number + 3]:
+            copy.start()
+
+    grad_q, grad_k = split_pair(reda[:, :QK])
+    grad_o, grad_v = split_pair(reda[:, QK : 2 * QK])
+    grad_kb, grad_qb = split_pair(reda[:, 2 * QK :])
+    update(0, enumerate((grad_q, grad_k, grad_v, grad_qb, grad_kb)), rate_matrix, decay_matrix)
+    update(1, [(Ellipsis, grad_o.T)], rate_matrix, decay_matrix)
+    update(2, [(Ellipsis, redf[:, :D])], rate_matrix, decay_matrix)
+    update(3, [(Ellipsis, redf[:, D:])], rate_matrix, decay_matrix)
+    update(4, [(Ellipsis, nred[0:4, : held[12].shape[1]])], rate_norm, 0.0)
+    for copy in copies + writes:
+        copy.wait()
 
 
 def box_lanes():
     quarter = D // 4
-    ladder = jnp.arange(quarter).astype(F32)
-    frequency = jnp.exp(ladder * (-math.log(10000.0) / quarter))
-    zero, one = jnp.zeros((quarter,), F32), jnp.ones((quarter,), F32)
-    return jnp.stack(
-        [
-            jnp.concatenate([frequency] * 4),
-            jnp.concatenate([zero, zero, one, one]),
-            jnp.concatenate([zero, one, zero, one]),
-        ]
-        + [jnp.zeros((D,), F32)] * 5
-    )
+    place = np.arange(D)
+    rows = np.zeros((8, D), np.float32)
+    rows[0] = np.exp((place % quarter) * (-math.log(10000.0) / quarter))
+    rows[1] = place >= 2 * quarter
+    rows[2] = place // quarter % 2
+    return jnp.asarray(rows)
 
 
 def per_device(
@@ -839,25 +964,16 @@
     chunks = tokens // SEQ
     share = attn_in.shape[1]
     ring = devices // 2 if devices % 4 == 0 and share % 32 == 0 else 0
-    low_in = attn_in.astype(BF16)
-    packa = jnp.concatenate(
-        [
-            interleave(low_in[0], low_in[1]),
-            interleave(attn_out.T.astype(BF16), low_in[2]),
-            interleave(low_in[4], low_in[3]),
-        ],
-        axis=1,
-    )
-    packf = jnp.concatenate([ffn_in.astype(BF16), ffn_out.T.astype(BF16)], axis=1)
-    pnorm = jnp.pad(norm_weight, ((0, 4), (0, -share % 128)))
+    weights = (attn_in, attn_out, ffn_in, ffn_out.T, norm_weight)
     if not ring:
-        packa = lax.all_gather(packa, "dp", axis=0, tiled=True)
-        packf = lax.all_gather(packf, "dp", axis=0, tiled=True)
+        packf = jnp.concatenate([ffn_in.astype(BF16), ffn_out.T.astype(BF16)], axis=1)
         pnorm = lax.all_gather(norm_weight, "dp", axis=1, tiled=True)
-        pnorm = jnp.pad(pnorm, ((0, 4), (0, 0)))
-    pages = page_ids.astype(F32)
-    cols = jnp.stack([boxes[:, 0].astype(F32), boxes[:, 1].astype(F32), pages], axis=1)
-    keyrow = jnp.where(pad_mask == 0, pages, -1.0).reshape(chunks, 1, SEQ)
+        weights = (
+            lax.all_gather(pack_attention(attn_in, attn_out), "dp", axis=0, tiled=True),
+            lax.all_gather(packf, "dp", axis=0, tiled=True),
+            jnp.pad(pnorm, ((0, 4), (0, 0))),
+        )
+    pages, padding = (part.reshape(tokens // 128, 128) for part in (page_ids, pad_mask))
     count = max(ring, 1)
     any_space = pl.BlockSpec(memory_space=pl.ANY)
     inner = share if ring else 16
@@ -874,15 +990,18 @@
             jax.ShapeDtypeStruct((tokens, D), F32),
             jax.ShapeDtypeStruct((share if ring else D, ATT), F32),
             jax.ShapeDtypeStruct((share if ring else D, FFN), F32),
-            jax.ShapeDtypeStruct((8, D), F32),
+            jax.ShapeDtypeStruct((8, max(share, 128)) if ring else (8, D), F32),
         ),
-        in_specs=[vmem()] * 7 + [any_space],
+        in_specs=[any_space] + [vmem()] * 4 + [(vmem(),) * len(weights), any_space],
         out_specs=(any_space,) * 2 + (vmem() if ring else any_space,) * 2 + (vmem(),),
         scratch_shapes=[
             pltpu.VMEM((D, ATT), BF16),
             pltpu.VMEM((D, FFN), BF16),
-            pltpu.VMEM((2 * count,) + pnorm.shape, F32),
+            pltpu.VMEM((2 * count, 8, max(share, 128)), F32),
             pltpu.VMEM((8, D), F32),
+            pltpu.VMEM((8, tokens), F32),
+            pltpu.VMEM((tokens, 128), F32),
+            tile,
             pltpu.VMEM((D, D), BF16),
             pltpu.VMEM((D, QK), BF16),
             wide,
@@ -916,42 +1035,45 @@
             pltpu.VMEM((2, chunks, HALF, D), BF16),
             pltpu.SemaphoreType.REGULAR,
         ]
-        + [dma(3, count)] * 4
+        + [dma(3, 2, count)]
+        + [dma(3, count)] * 3
         + [dma(2, chunks)] * 4
         + [dma(3, chunks)] * 2
         + [dma(2, chunks)] * 3
         + [dma(chunks)]
         + [dma(count + 1)] * 2
+        + [pltpu.SemaphoreType.DMA]
         + [dma(2, count)] * 4,
         compiler_params=pltpu.CompilerParams(
             collective_id=0, has_side_effects=True, vmem_limit_bytes=VMEM_LIMIT
         ),
-    )(hidden_in, cols, keyrow, box_lanes(), packa, packf, pnorm, out_grad)
-    redup, reddown = redf[:, :D], redf[:, D:]
-    position = lax.axis_index("dp")
+    )(hidden_in, boxes.T, pages, padding, box_lanes(), weights, out_grad)
     if not ring:
-        reda, redup, reddown = (
-            lax.psum_scatter(part, "dp", scatter_dimension=0, tiled=True)
-            for part in (reda, redup, reddown)
+        reda, redf = (
+            lax.psum_scatter(part, "dp", scatter_dimension=0, tiled=True) for part in (reda, redf)
         )
         nred = lax.psum(nred, ("dp", "mp")) * 0.5
-    grad_norm = lax.dynamic_slice_in_dim(nred[:4], position * share, share, 1)
-    grad_q, grad_k = split_pair(reda[:, :QK])
-    grad_o, grad_v = split_pair(reda[:, QK : 2 * QK])
-    grad_kb, grad_qb = split_pair(reda[:, 2 * QK :])
-    grad_in = jnp.stack([grad_q, grad_k, grad_v, grad_qb, grad_kb])
-    new_in = adam_step(
-        attn_in, grad_in, attn_in_moment, attn_in_second, rate_matrix, decay_matrix
+        nred = lax.dynamic_slice_in_dim(nred, lax.axis_index("dp") * share, share, 1)
+    old = (
+        (attn_in, attn_in_moment, attn_in_second)
+        + (attn_out, attn_out_moment, attn_out_second)
+        + (ffn_in, ffn_in_moment, ffn_in_second)
+        + (ffn_out.T, ffn_out_moment.T, ffn_out_second.T)
+        + (norm_weight, norm_moment, norm_second)
     )
-    new_out = adam_step(
-        attn_out, grad_o.T, attn_out_moment, attn_out_second, rate_matrix, decay_matrix
-    )
-    new_up = adam_step(ffn_in, redup, ffn_in_moment, ffn_in_second, rate_matrix, decay_matrix)
-    new_down = adam_step(
-        ffn_out, reddown.T, ffn_out_moment, ffn_out_second, rate_matrix, decay_matrix
-    )
-    new_norm = adam_step(norm_weight, grad_norm, norm_moment, norm_second, rate_norm, 0.0)
-    return (mixed, input_grad) + new_in + new_out + new_up + new_down + new_norm
+    large = (mixed, input_grad)
+    summed = (reda, redf, nred)
+    new = pl.pallas_call(
+        finish_kernel,
+        out_shape=tuple(jax.ShapeDtypeStruct(part.shape, part.dtype) for part in large + old),
+        in_specs=[any_space] * 20,
+        out_specs=(any_space,) * 17,
+        scratch_shapes=[pltpu.VMEM(part.shape, F32) for part in summed + old + old]
+        + [pltpu.VMEM(part.shape, part.dtype) for part in large]
+        + [dma(18), dma(15), dma(8), dma(8)],
+        compiler_params=pltpu.CompilerParams(vmem_limit_bytes=VMEM_LIMIT),
+    )(*summed, *large, *old)
+    return new[:11] + tuple(part.T for part in new[11:14]) + new[14:]
 
 
 def solution(mesh):

time: 218 us -> 192 us (0.88)
  local copies, waits for them, and re-layouts: 19 us -> 0 us
  other arithmetic: 12.2 us -> 0 us
  Pallas kernels: 185 us -> 191 us
    unnamed x34 -> x0, local copies, waits for them, and re-layouts: 12.6 us -> none
    pallas_call x0 -> x1, Pallas kernels: none -> 8.54 us  [per_device(): pl.pallas_call(finish_kernel, out_shape=tuple((jax.ShapeDtypeStruct(part....]
    sub x5 -> x0, other arithmetic: 8.21 us -> none  [adam_step(): weight - rate * (moment_hat / (jnp.sqrt(second_hat) + epsilon_adam) + dec...]
    pallas_call x1, Pallas kernels: 185 us -> 182 us  [per_device(): pl.pallas_call(partial(layer_kernel, ring, chunks), out_shape=(jax.ShapeD...]
    another operation x7 -> x0, local copies, waits for them, and re-layouts: 2.55 us -> none  [the longest x4 1.35 us: box_lanes(): jnp.stack([jnp.concatenate([frequency] * 4), jnp.concatenate([zero, zero,...]
    slice x9 -> x0, local copies, waits for them, and re-layouts: 2.22 us -> none  [the longest x2 1.26 us: per_device(): grad_kb, grad_qb = split_pair(reda[:, 2 * QK:])]
where the time goes in v3:
time: 192 us
  Pallas kernels  191 us (99%)
    pallas_call x1, Pallas kernels, per_device(): pl.pallas_call(partial(layer_kernel, ring, chunks), out_shape=(jax.ShapeD...  182 us
    pallas_call x1, Pallas kernels, per_device(): pl.pallas_call(finish_kernel, out_shape=tuple((jax.ShapeDtypeStruct(part....  8.54 us

profile of v3, /device:TPU:0, one launch (start us, length us, event | category | flops | bytes accessed | tf_op | source)
XLA Modules:
  0.0 191.8 jit_solution(18243246940557895047)
XLA Ops:
  0.7 182.4 %shard_map.332 = (bf16[1536,768]{1,0:T(8,128)(2,1)}, f32[1536,768]{1,0:T(8,128)}, f32[96,1152]{1,0:T(8,128)}, f32[96,1536]{1,0:T(8,128)}, f32[8,128]{1,0:T(8,128)}) custom-call(bf16[1536,768]{1,0:T(8,128)(2,1)} %hidden_hbm.1, s32[2,1536]{1,0:T(2,128)} %bitcast.13, s32[12,128]{1,0:T(8,128)} %bitcast.14, s32[12,128]{1,0:T(8,128)} %bitcast.15, ...), custom_call_target="tpu_custom_call" | custom-call | tf_op jit(solution)/shard_map/pallas_call | solution.py:986
  183.1 8.5 %shard_map.333 = (bf16[1536,768]{1,0:T(8,128)(2,1)}, f32[1536,768]{1,0:T(8,128)}, f32[5,96,192]{2,1,0:T(8,128)}, f32[5,96,192]{2,1,0:T(8,128)}, f32[5,96,192]{2,...) custom-call(f32[96,1152]{1,0:T(8,128)} %get-tuple-element.39.refs_0_, ...), custom_call_target="tpu_custom_call" | custom-call | tf_op jit(solution)/shard_map/pallas_call | solution.py:1066

commit v4 on v3

--- a/solution.py
+++ b/solution.py
@@ -196,10 +196,18 @@
         self.psend[r] = value.astype(BF16)
         self.to_pair(r).start()
 
-    def keep(self, r, value):
+    def hold(self, r, value):
+        self.sums[r] = value.astype(BF16)
+
+    def keep(self, r):
         self.to_pair(r).wait_recv()
-        self.sums[r] = (value + self.precv[r].astype(F32)).astype(BF16)
+        self.sums[r] = (self.sums[r].astype(F32) + self.precv[r].astype(F32)).astype(BF16)
         self.over(r).start()
+
+    def keep_last(self, r):
+        @pl.when(r > 0)
+        def _():
+            self.keep(r - 1)
 
     def wait(self, r):
         self.over(r).wait_recv()
@@ -265,8 +273,8 @@
 
 
 class Scatter:
-    def __init__(self, place, share, src, width, xsend, xrecv, zsend, zrecv, sems):
-        self.p, self.share, self.src, self.width = place, share, src, width
+    def __init__(self, place, share, src, cols, xsend, xrecv, zsend, zrecv, sems):
+        self.p, self.share, self.src, self.cols = place, share, src, cols
         self.xsend, self.xrecv, self.zsend, self.zrecv = xsend, xrecv, zsend, zrecv
         self.xs, self.xr, self.zs, self.zr = sems
 
@@ -276,8 +284,8 @@
 
     def xcopy(self, k):
         return remote(
-            self.xsend.at[k, :, : self.width],
-            self.xrecv.at[k],
+            self.xsend.at[k, :, self.cols],
+            self.xrecv.at[k, :, self.cols],
             self.xs.at[k],
             self.xr.at[k],
             self.p.xdev,
@@ -285,27 +293,29 @@
 
     def zcopy(self, k):
         return remote(
-            self.zsend.at[k, :, : self.width],
-            self.zrecv.at[k],
+            self.zsend.at[k - 1, :, self.cols],
+            self.zrecv.at[k - 1, :, self.cols],
             self.zs.at[k],
             self.zr.at[k],
             self.p.zdev(k),
         )
 
     def start(self, k):
-        value = self.src[self.rows(k, 1 - self.p.x), : self.width]
-        self.xsend[k, :, : self.width] = value.astype(BF16)
+        value = self.src[self.rows(k, 1 - self.p.x), self.cols]
+        self.xsend[k, :, self.cols] = value.astype(BF16)
         self.xcopy(k).start()
 
+    def added(self, k):
+        self.xcopy(k).wait_recv()
+        mine = self.src[self.rows(k, self.p.x), self.cols]
+        return mine + self.xrecv[k, :, self.cols].astype(F32)
+
     def middle(self, k):
-        self.xcopy(k).wait_recv()
-        value = self.src[self.rows(k, self.p.x), : self.width] + self.xrecv[k].astype(F32)
-        self.zsend[k, :, : self.width] = value.astype(BF16)
+        self.zsend[k - 1, :, self.cols] = self.added(k).astype(BF16)
         self.zcopy(k).start()
 
     def own(self, out):
-        self.xcopy(0).wait_recv()
-        out[...] = self.src[self.rows(0, self.p.x), : self.width] + self.xrecv[0].astype(F32)
+        out[:, self.cols] = self.added(0)
 
     def sent(self):
         for k in range(self.p.ring):
@@ -314,11 +324,11 @@
             self.zcopy(k).wait_send()
 
     def finish(self, out):
-        value = out[...]
+        value = out[:, self.cols]
         for k in range(1, self.p.ring):
             self.zcopy(k).wait_recv()
-            value = value + self.zrecv[k].astype(F32)
-        out[...] = value
+            value = value + self.zrecv[k - 1, :, self.cols].astype(F32)
+        out[:, self.cols] = value
 
 
 def layer_kernel(
@@ -368,6 +378,8 @@
     zsend,
     fxrecv,
     fzrecv,
+    axsend,
+    azsend,
     axrecv,
     azrecv,
     psend,
@@ -488,10 +500,6 @@
         rk[rows, :] = jnp.where(low, box, text[:, :QK]).astype(BF16)
         vk[rows, :] = text[:, QK:].astype(BF16)
 
-    steps(tokens, HALF, project)
-    if ring > 2:
-        gather_f.step(2)
-        gather_n.step(2)
     scores = big.at[:HALF, :SEQ]
     pre = big.at[:HALF, :]
     dprob = big.at[:, :SEQ]
@@ -519,23 +527,24 @@
             ctx[q_rows, tile] = jnp.where(low, pltpu.roll(found, HEAD_DIM, 1), 0.0).astype(BF16)
         return dot_nt(ctx[q_rows, :], wa[:, QK : 2 * QK])
 
-    spread = ring - 1 == chunks
-
     def stage_a(r, carry):
+        project(pl.multiple_of(r * SEQ, SEQ))
+        project(pl.multiple_of(r * SEQ + HALF, HALF))
         sum_a.give(r, attend(r, 1 - p.half))
-        sum_a.keep(r, attend(r, p.half))
+        sum_a.hold(r, attend(r, p.half))
+        sum_a.keep(r)
         if ring > 3:
 
-            @pl.when(r == 0)
+            @pl.when(r < 2)
             def _():
-                gather_f.step(3)
-                gather_n.step(3)
+                gather_f.step(r + 2)
+                gather_n.step(r + 2)
 
         return carry
 
     lax.fori_loop(0, chunks, stage_a, 0)
     if ring:
-        for s in range(4, ring):
+        for s in range(4 if ring > 3 and chunks > 1 else 2 + (ring > 3), ring):
             gather_f.step(s)
             gather_n.step(s)
         gather_n.finish()
@@ -584,12 +593,14 @@
         steps(HALF, 128, part)
         pass_on(shared, 0, p.own(r), r).start()
         sum_a.close(r)
+        sum_b.keep_last(r)
+        sum_b.hold(r, up_down(own_at(r)))
         pass_on(shared, 0, p.other(r), r).wait_recv()
         sum_b.give(r, up_down(other_at(r)))
-        sum_b.keep(r, up_down(own_at(r)))
         return carry
 
     lax.fori_loop(0, chunks, stage_b, 0)
+    sum_b.keep(chunks - 1)
     nsum[...] = jnp.zeros_like(nsum)
 
     def mixed_here(r):
@@ -609,6 +620,43 @@
 
         steps(HALF, 64, times)
         return dot_nt(slope[rows, :], wf[:, :D])
+
+    if ring:
+        scatter_sems = (sxs, sxr, szs, szr)
+        scatter_up, scatter_down, scatter_a = (
+            Scatter(p, share, src, cols_of, *held, [part.at[number] for part in scatter_sems])
+            for number, (src, cols_of, held) in enumerate(
+                (
+                    (grads, slice(0, D), (xsend, fxrecv, zsend, fzrecv)),
+                    (grads, slice(D, FFN), (xsend, fxrecv, zsend, fzrecv)),
+                    (grads, slice(0, ATT), (axsend, axrecv, azsend, azrecv)),
+                )
+            )
+        )
+    else:
+        scatter_up = scatter_down = scatter_a = None
+    block = 4 * share if ring else D // 2
+
+    def weight_blocks(work, scatter):
+        def run(i, carry):
+            place = (p.z // 2 + 1 + i) % (ring // 2) if ring else i
+            work(pl.ds(pl.multiple_of(place * block, block), block))
+            if ring:
+                far = 1 - p.z % 2
+                for line in (far, 1 - far):
+                    scatter.start((2 * place + line + ring - p.z) % ring)
+            return carry
+
+        lax.fori_loop(0, D // block, run, 0)
+
+    def up_weights(rows):
+        grads[rows, :D] = grad_of(shared, rows, slope)
+
+    def down_weights(rows):
+        grads[rows, D:] = grad_of(low_two, rows, active)
+
+    def grad_of(left, rows, right):
+        return dot_tn(left[:, rows], right[...])
 
     def stage_c(r, carry):
         ograd_copy(r).wait()
@@ -632,42 +680,20 @@
         mixed_here(r).start()
         mixed_pair(p.own(r), r).start()
         sum_b.close(r)
+        sum_c.keep_last(r)
+        sum_c.hold(r, back(own_at(r)))
         pass_on(low_two, 1, p.other(r), r).wait_recv()
+
+        @pl.when(r == chunks - 1)
+        def _():
+            weight_blocks(down_weights, scatter_down)
+
         sum_c.give(r, back(other_at(r)))
-        sum_c.keep(r, back(own_at(r)))
         return carry
 
     lax.fori_loop(0, chunks, stage_c, 0)
-    if ring:
-        scatter_sems = (sxs, sxr, szs, szr)
-        scatter_f = Scatter(
-            p, share, grads, FFN, xsend, fxrecv, zsend, fzrecv, [s.at[0] for s in scatter_sems]
-        )
-        scatter_a = Scatter(
-            p, share, grads, ATT, xsend, axrecv, zsend, azrecv, [s.at[1] for s in scatter_sems]
-        )
-    block = 4 * share if ring else D // 2
-
-    def weight_blocks(work, scatter):
-        def run(i, carry):
-            place = (p.z // 2 + 1 + i) % (ring // 2) if ring else i
-            work(pl.ds(pl.multiple_of(place * block, block), block))
-            if ring:
-                far = 1 - p.z % 2
-                for line in (far, 1 - far):
-                    scatter.start((2 * place + line + ring - p.z) % ring)
-            return carry
-
-        lax.fori_loop(0, D // block, run, 0)
-
-    def ffn_weights(rows):
-        grads[rows, :D] = grad_of(shared, rows, slope)
-        grads[rows, D:] = grad_of(low_two, rows, active)
-
-    def grad_of(left, rows, right):
-        return dot_tn(left[:, rows], right[...])
-
-    weight_blocks(ffn_weights, scatter_f if ring else None)
+    weight_blocks(up_weights, scatter_up)
+    sum_c.keep(chunks - 1)
 
     def settle(r, carry):
         pass_on(shared, 0, p.own(r), r).wait_send()
@@ -682,11 +708,13 @@
     gctx, gscore = slope.at[:SEQ, QK:], low_two.at[:SEQ, :SEQ]
     score_scale = HEAD_DIM**-0.5
 
+    def context_back(r, side):
+        rows = pl.ds(pl.multiple_of(r * SEQ + side * HALF, HALF), HALF)
+        there = pl.ds(pl.multiple_of(side * HALF, HALF), HALF)
+        gctx[there, :] = dot(low_one[rows, :], wop[...]).astype(BF16)
+
     def attend_back(r):
         k_rows = pl.ds(pl.multiple_of(r * SEQ, SEQ), SEQ)
-        for side in range(2):
-            rows = pl.ds(pl.multiple_of(r * SEQ + side * HALF, HALF), HALF)
-            gctx[side * HALF : (side + 1) * HALF, :] = dot(low_one[rows, :], wop[...]).astype(BF16)
         low = lower_half((SEQ, 128))
         for h in range(HEADS):
             tile = slice(h * 128, (h + 1) * 128)
@@ -731,21 +759,28 @@
         steps(HALF, 128, part)
         pass_on(low_one, 2, p.own(r), r).start()
         sum_c.close(r)
+        sum_d.keep_last(r)
+        context_back(r, p.half)
         pass_on(low_one, 2, p.other(r), r).wait_recv()
+        context_back(r, 1 - p.half)
+        if ring:
+
+            @pl.when(r == min(1, chunks - 1))
+            def _():
+                for k in range(1, ring):
+                    scatter_down.middle(k)
+
+            @pl.when(r == chunks - 1)
+            def _():
+                for k in range(1, ring):
+                    scatter_up.middle(k)
+
         attend_back(r)
         sum_d.give(r, partial_of(p.other(r)))
-        sum_d.keep(r, partial_of(p.own(r)))
-        if spread:
-            scatter_f.middle(r + 1)
+        sum_d.hold(r, partial_of(p.own(r)))
         return carry
 
     lax.fori_loop(0, chunks, stage_d, 0)
-    if ring:
-        if not spread:
-            for k in range(1, ring):
-                scatter_f.middle(k)
-        scatter_f.own(outf)
-        scatter_f.sent()
 
     def attention_weights(rows):
         text = grad_of(hidden, rows, gtext)
@@ -753,7 +788,11 @@
         grads[rows, QK : 2 * QK] = text[:, QK:] + grad_of(low_one, rows, ctx)
         grads[rows, 2 * QK : ATT] = grad_of(emb, rows, gbox)
 
-    weight_blocks(attention_weights, scatter_a if ring else None)
+    if ring:
+        scatter_down.own(outf)
+        scatter_up.own(outf)
+    weight_blocks(attention_weights, scatter_a)
+    sum_d.keep(chunks - 1)
     for row in range(4):
         nsum[row : row + 1, :] = jnp.sum(nsum[row * 8 : row * 8 + 8, :], axis=0, keepdims=True)
     if ring:
@@ -801,9 +840,11 @@
     if ring:
         for gather in (gather_a, gather_f, gather_n):
             gather.drain()
-        scatter_f.finish(outf)
+        scatter_down.finish(outf)
+        scatter_up.finish(outf)
         scatter_a.finish(outa)
-        scatter_a.sent()
+        for scatter in (scatter_down, scatter_up, scatter_a):
+            scatter.sent()
         summed = nsum[16:24, :]
         for k in range(1, ring):
             norm_z[k - 1].wait_recv()
@@ -983,6 +1024,8 @@
     own_low = pltpu.VMEM((chunks, HALF, D), BF16)
     att_share = pltpu.VMEM((count, inner, ATT), BF16)
     ffn_share = pltpu.VMEM((count, inner, FFN), BF16)
+    att_along = pltpu.VMEM((max(count - 1, 1), inner, ATT), BF16)
+    ffn_along = pltpu.VMEM((max(count - 1, 1), inner, FFN), BF16)
     mixed, input_grad, reda, redf, nred = pl.pallas_call(
         partial(layer_kernel, ring, chunks),
         out_shape=(
@@ -1024,11 +1067,13 @@
             pltpu.VMEM((32, D), F32),
             pltpu.VMEM((count + 1, 8, D), F32),
             ffn_share,
+            ffn_along,
             ffn_share,
-            ffn_share,
-            ffn_share,
+            ffn_along,
             att_share,
+            att_along,
             att_share,
+            att_along,
             own_low,
             own_low,
             own_low,
@@ -1043,7 +1088,7 @@
         + [dma(chunks)]
         + [dma(count + 1)] * 2
         + [pltpu.SemaphoreType.DMA]
-        + [dma(2, count)] * 4,
+        + [dma(3, count)] * 4,
         compiler_params=pltpu.CompilerParams(
             collective_id=0, has_side_effects=True, vmem_limit_bytes=VMEM_LIMIT
         ),

time: 192 us -> 172 us (0.90)
  Pallas kernels: 191 us -> 171 us
    pallas_call x1, Pallas kernels: 182 us -> 163 us  [per_device(): pl.pallas_call(partial(layer_kernel, ring, chunks), out_shape=(jax.ShapeD...]
where the time goes in v4:
time: 172 us
  Pallas kernels  171 us (99%)
    pallas_call x1, Pallas kernels, per_device(): pl.pallas_call(partial(layer_kernel, ring, chunks), out_shape=(jax.ShapeD...  163 us
    pallas_call x1, Pallas kernels, per_device(): pl.pallas_call(finish_kernel, out_shape=tuple((jax.ShapeDtypeStruct(part....  8.54 us

profile of v4, /device:TPU:0, one launch (start us, length us, event | category | flops | bytes accessed | tf_op | source)
XLA Modules:
  0.0 172.1 jit_solution(12058079310649625478)
XLA Ops:
  0.7 162.8 %shard_map.332 = (bf16[1536,768]{1,0:T(8,128)(2,1)}, f32[1536,768]{1,0:T(8,128)}, f32[96,1152]{1,0:T(8,128)}, f32[96,1536]{1,0:T(8,128)}, f32[8,128]{1,0:T(8,128)}) custom-call(bf16[1536,768]{1,0:T(8,128)(2,1)} %hidden_hbm.1, s32[2,1536]{1,0:T(2,128)} %bitcast.13, s32[12,128]{1,0:T(8,128)} %bitcast.14, s32[12,128]{1,0:T(8,128)} %bitcast.15, ...), custom_call_target="tpu_custom_call" | custom-call | tf_op jit(solution)/shard_map/pallas_call | solution.py:1029
  163.4 8.5 %shard_map.333 = (bf16[1536,768]{1,0:T(8,128)(2,1)}, f32[1536,768]{1,0:T(8,128)}, f32[5,96,192]{2,1,0:T(8,128)}, f32[5,96,192]{2,1,0:T(8,128)}, f32[5,96,192]{2,...) custom-call(f32[96,1152]{1,0:T(8,128)} %get-tuple-element.39.refs_0_, ...), custom_call_target="tpu_custom_call" | custom-call | tf_op jit(solution)/shard_map/pallas_call | solution.py:1111

commit v5 on v4

--- a/solution.py
+++ b/solution.py
@@ -75,6 +75,7 @@
         self.half = self.mp % 2
         self.pair = (self.dp, self.mp + 1 - 2 * self.half)
         self.across = (self.dp, (self.mp + 2) % 4)
+        self.diagonal = (self.dp, (self.mp + 2) % 4 + 1 - 2 * self.half)
         self.ring = ring
         self.z = self.dp // 2
         self.x = self.dp % 2
@@ -84,7 +85,7 @@
         return (((self.z + k) % self.ring) * 2 + self.x, self.mp)
 
     def greet(self):
-        peers = [self.pair, self.across]
+        peers = [self.pair, self.across, self.diagonal]
         if self.ring:
             peers += [self.xdev] + [self.zdev(k) for k in range(1, self.ring)]
         barrier = pltpu.get_barrier_semaphore()
@@ -355,6 +356,7 @@
     hidden,
     wtx,
     wop,
+    wo,
     lq,
     rk,
     vk,
@@ -404,6 +406,10 @@
     ns,
     nr,
     hs,
+    ctx_s,
+    ctx_r,
+    wo_s,
+    wo_r,
     sxs,
     sxr,
     szs,
@@ -420,9 +426,8 @@
     for r in range(chunks):
         ograd_copy(r).start()
     sums_sems = (ps, pr, ys, yr)
-    sum_a, sum_b, sum_c, sum_d = (
-        Sum(p, stage_number % 2, psend, precv, sums, yrecv, sums_sems)
-        for stage_number in range(4)
+    sum_b, sum_c, sum_d = (
+        Sum(p, number % 2, psend, precv, sums, yrecv, sums_sems) for number in range(3)
     )
     if ring:
         attn_in, attn_out, ffn_in, ffn_out, norm_in = weights
@@ -480,31 +485,63 @@
     def build(row):
         rows = pl.ds(row, 256)
         low = lower_half((256, 128))
-        wtx[rows, :QK] = wa[rows, :QK]
         for h in range(HEADS):
             qk_cols = slice(h * 128, (h + 1) * 128)
             ov_cols = slice(QK + h * 128, QK + (h + 1) * 128)
             ov = wa[rows, ov_cols].astype(F32)
-            wtx[rows, ov_cols] = jnp.where(low, rolled(wa[rows, qk_cols]), ov).astype(BF16)
+            wtx[rows, h * 256 : h * 256 + 128] = wa[rows, qk_cols]
+            wtx[rows, h * 256 + 128 : h * 256 + 256] = jnp.where(
+                low, rolled(wa[rows, qk_cols]), ov
+            ).astype(BF16)
             wop[rows, qk_cols] = jnp.where(low, 0.0, rolled(ov)).astype(BF16)
+        first, second, third = (
+            wa[rows, QK + h * 128 : QK + (h + 1) * 128].astype(F32) for h in range(HEADS)
+        )
+        wo[row // 256, :, :128] = jnp.where(low, first, rolled(second)).astype(BF16)
+        wo[row // 256, :, 128:] = jnp.where(low, third, 0.0).astype(BF16)
 
     steps(D, 256, build)
+
+    def wo_slot(k):
+        return stage.at[0 : D // 256, :, k * 256 : (k + 1) * 256]
+
+    def wo_copy(k):
+        if k == 2:
+            return remote(wo_slot(1), wo_slot(2), wo_s.at[2], wo_r.at[2], p.pair)
+        return remote(wo, wo_slot(k), wo_s.at[k], wo_r.at[k], (p.pair, p.across)[k])
+
+    wo_copy(1).start()
+    wo_copy(0).start()
     hidden_copy.wait()
 
     def project(row):
         rows = pl.ds(row, HALF)
         text = dot(hidden[rows, :], wtx[...])
         box = dot(emb[rows, :], wa[:, 2 * QK :])
-        low = lower_half((HALF, QK))
-        lq[rows, :] = jnp.where(low, text[:, :QK], box).astype(BF16)
-        rk[rows, :] = jnp.where(low, box, text[:, :QK]).astype(BF16)
-        vk[rows, :] = text[:, QK:].astype(BF16)
+        low = lower_half((HALF, 128))
+        for h in range(HEADS):
+            tile = slice(h * 128, (h + 1) * 128)
+            word, extra = text[:, h * 256 : h * 256 + 128], box[:, tile]
+            lq[rows, tile] = jnp.where(low, word, extra).astype(BF16)
+            rk[rows, tile] = jnp.where(low, extra, word).astype(BF16)
+            vk[rows, tile] = text[:, h * 256 + 128 : h * 256 + 256].astype(BF16)
 
     scores = big.at[:HALF, :SEQ]
-    pre = big.at[:HALF, :]
+    pre, post = big.at[:HALF, :], big.at[HALF:, :]
     dprob = big.at[:, :SEQ]
 
-    def attend(r, side):
+    def ctx_kept(r, own):
+        rows = pl.ds(pl.multiple_of(r * SEQ + HALF, HALF), HALF)
+        return active.at[rows, 256:512] if own else active.at[rows, 0:256]
+
+    def ctx_copy(k, r):
+        rows = pl.ds(pl.multiple_of(r * SEQ, HALF), HALF)
+        peer = (p.pair, p.across, p.diagonal)[k]
+        slot = active.at[rows, k * 256 : (k + 1) * 256]
+        return remote(ctx_kept(r, k == 1), slot, ctx_s.at[k, r], ctx_r.at[k, r], peer)
+
+    def attend(r, side, kept):
+        found = []
         start = pl.multiple_of(side * HALF, HALF)
         q_rows = pl.ds(pl.multiple_of(r * SEQ + start, HALF), HALF)
         k_rows = pl.ds(pl.multiple_of(r * SEQ, SEQ), SEQ)
@@ -523,16 +560,28 @@
             raised = jnp.exp(value - jnp.max(value, axis=-1, keepdims=True))
             value = raised / jnp.sum(raised, axis=-1, keepdims=True)
             probs[r, h, pl.ds(start, HALF), :] = value.astype(BF16)
-            found = dot(probs[r, h, pl.ds(start, HALF), :], vk[k_rows, tile])
-            ctx[q_rows, tile] = jnp.where(low, pltpu.roll(found, HEAD_DIM, 1), 0.0).astype(BF16)
-        return dot_nt(ctx[q_rows, :], wa[:, QK : 2 * QK])
+            found.append(dot(probs[r, h, pl.ds(start, HALF), :], vk[k_rows, tile]))
+            turned = pltpu.roll(found[h], HEAD_DIM, 1)
+            ctx[q_rows, tile] = jnp.where(low, turned, 0.0).astype(BF16)
+            if h == 0:
+                even = turned
+        kept[:, :128] = jnp.where(low, even, found[1]).astype(BF16)
+        kept[:, 128:] = ctx[q_rows, 256:384]
 
     def stage_a(r, carry):
         project(pl.multiple_of(r * SEQ, SEQ))
         project(pl.multiple_of(r * SEQ + HALF, HALF))
-        sum_a.give(r, attend(r, 1 - p.half))
-        sum_a.hold(r, attend(r, p.half))
-        sum_a.keep(r)
+        attend(r, 1 - p.half, ctx_kept(r, False))
+        ctx_copy(2, r).start()
+        ctx_copy(0, r).start()
+        attend(r, p.half, ctx_kept(r, True))
+        ctx_copy(1, r).start()
+
+        @pl.when(r == 0)
+        def _():
+            wo_copy(1).wait_recv()
+            wo_copy(2).start()
+
         if ring > 3:
 
             @pl.when(r < 2)
@@ -579,20 +628,33 @@
     def other_at(r):
         return pl.multiple_of(r * SEQ + (1 - p.half) * HALF, HALF)
 
+    wo_copy(0).wait_recv()
+    wo_copy(2).wait_recv()
+    for k in range(3):
+        wo_copy(k).wait_send()
+
     def stage_b(r, carry):
-        sum_a.wait(r)
+        for k in range(3):
+            ctx_copy(k, r).wait_recv()
+        theirs = active[pl.ds(pl.multiple_of(r * SEQ, HALF), HALF), :]
+        mine = ctx_kept(r, True)[...]
+        for j in range(D // 256):
+            cut = [dot_nt(theirs[:, k * 256 : k * 256 + 256], wo_slot(k)[j]) for k in range(3)]
+            pre[:, j * 256 : (j + 1) * 256] = dot_nt(mine, wo[j]) + cut[0]
+            post[:, j * 256 : (j + 1) * 256] = cut[1] + cut[2]
 
         def part(row):
             rows = pl.ds(pl.multiple_of(own_at(r) + row, 128), 128)
             here = pl.ds(row, 128)
-            normal, scale = norm_of(hidden[rows, :].astype(F32) + sum_a.total(r, here))
+            normal, scale = norm_of(hidden[rows, :].astype(F32) + (pre[here, :] + post[here, :]))
             xone[r, here, :] = normal
             rone[r, here, :] = jnp.broadcast_to(scale, (128, 128))
             shared[rows, :] = (normal * gain_one + bias_one).astype(BF16)
 
         steps(HALF, 128, part)
         pass_on(shared, 0, p.own(r), r).start()
-        sum_a.close(r)
+        for k in range(3):
+            ctx_copy(k, r).wait_send()
         sum_b.keep_last(r)
         sum_b.hold(r, up_down(own_at(r)))
         pass_on(shared, 0, p.other(r), r).wait_recv()
@@ -623,18 +685,22 @@
 
     if ring:
         scatter_sems = (sxs, sxr, szs, szr)
-        scatter_up, scatter_down, scatter_a = (
+        held = (axsend, axrecv, azsend, azrecv)
+        scatter_up, scatter_down, *scatter_heads = (
             Scatter(p, share, src, cols_of, *held, [part.at[number] for part in scatter_sems])
             for number, (src, cols_of, held) in enumerate(
                 (
                     (grads, slice(0, D), (xsend, fxrecv, zsend, fzrecv)),
                     (grads, slice(D, FFN), (xsend, fxrecv, zsend, fzrecv)),
-                    (grads, slice(0, ATT), (axsend, axrecv, azsend, azrecv)),
+                    (grads, slice(0, QK), held),
+                    (grads, slice(QK, 2 * QK), held),
+                    (grads, slice(2 * QK, ATT), held),
                 )
             )
         )
     else:
-        scatter_up = scatter_down = scatter_a = None
+        scatter_up = scatter_down = None
+        scatter_heads = [None] * HEADS
     block = 4 * share if ring else D // 2
 
     def weight_blocks(work, scatter):
@@ -708,6 +774,13 @@
     gctx, gscore = slope.at[:SEQ, QK:], low_two.at[:SEQ, :SEQ]
     score_scale = HEAD_DIM**-0.5
 
+    def attention_weights(h, rows):
+        at, tile = h * QK, slice(h * 128, (h + 1) * 128)
+        text = grad_of(hidden, rows, gtext.at[:, h * 256 : (h + 1) * 256])
+        grads[rows, at : at + 128] = text[:, :128]
+        grads[rows, at + 128 : at + 256] = text[:, 128:] + grad_of(low_one, rows, ctx.at[:, tile])
+        grads[rows, at + 256 : at + 384] = grad_of(emb, rows, gbox.at[:, tile])
+
     def context_back(r, side):
         rows = pl.ds(pl.multiple_of(r * SEQ + side * HALF, HALF), HALF)
         there = pl.ds(pl.multiple_of(side * HALF, HALF), HALF)
@@ -721,21 +794,26 @@
             dprob[...] = dot_nt(gctx[:, tile], vk[k_rows, tile])
 
             def soften(row):
-                rows = pl.ds(row, 256)
+                rows = pl.ds(row, SEQ)
                 grad = dprob[rows, :]
                 prob = probs[r, h, rows, :].astype(F32)
                 weighted = jnp.sum(prob * grad, axis=-1, keepdims=True)
                 gscore[rows, :] = (prob * (grad - weighted)).astype(BF16)
 
-            steps(SEQ, 256, soften)
+            steps(SEQ, SEQ, soften)
             left = dot(gscore[...], rk[k_rows, tile]) * score_scale
             right = dot_tn(gscore[...], lq[k_rows, tile]) * score_scale
             value = dot_tn(probs[r, h], gctx[:, tile])
-            gtext[k_rows, tile] = jnp.where(
+            gtext[k_rows, h * 256 : h * 256 + 128] = jnp.where(
                 low, left + pltpu.roll(left, HEAD_DIM, 1), right + pltpu.roll(right, HEAD_DIM, 1)
             ).astype(BF16)
             gbox[k_rows, tile] = jnp.where(low, right, left).astype(BF16)
-            gtext[k_rows, QK + h * 128 : QK + (h + 1) * 128] = value.astype(BF16)
+            gtext[k_rows, h * 256 + 128 : h * 256 + 256] = value.astype(BF16)
+
+            @pl.when(r == chunks - 1)
+            def _():
+                weight_blocks(partial(attention_weights, h), scatter_heads[h])
+
 
     def partial_of(rows):
         return dot_nt(gtext[rows, :], wtx[...])
@@ -774,6 +852,8 @@
             def _():
                 for k in range(1, ring):
                     scatter_up.middle(k)
+                scatter_down.own(outf)
+                scatter_up.own(outf)
 
         attend_back(r)
         sum_d.give(r, partial_of(p.other(r)))
@@ -782,30 +862,23 @@
 
     lax.fori_loop(0, chunks, stage_d, 0)
 
-    def attention_weights(rows):
-        text = grad_of(hidden, rows, gtext)
-        grads[rows, :QK] = text[:, :QK]
-        grads[rows, QK : 2 * QK] = text[:, QK:] + grad_of(low_one, rows, ctx)
-        grads[rows, 2 * QK : ATT] = grad_of(emb, rows, gbox)
-
-    if ring:
-        scatter_down.own(outf)
-        scatter_up.own(outf)
-    weight_blocks(attention_weights, scatter_a)
     sum_d.keep(chunks - 1)
     for row in range(4):
         nsum[row : row + 1, :] = jnp.sum(nsum[row * 8 : row * 8 + 8, :], axis=0, keepdims=True)
     if ring:
         norm_pair = remote(nsum.at[0:8], nrecv.at[0], ns.at[0], nr.at[0], p.pair)
         norm_pair.start()
-        scatter_a.middle(1)
+        for k in range(1, ring):
+            scatter_heads[0].middle(k)
         norm_pair.wait_recv()
         nsum[8:16, :] = nsum[0:8, :] + nrecv[0]
         norm_x = remote(nsum.at[8:16], nrecv.at[1], ns.at[1], nr.at[1], p.xdev)
         norm_x.start()
-        for k in range(2, ring):
-            scatter_a.middle(k)
-        scatter_a.own(outa)
+        for scatter in scatter_heads[1:]:
+            for k in range(1, ring):
+                scatter.middle(k)
+        for scatter in scatter_heads:
+            scatter.own(outa)
         norm_x.wait_recv()
         nsum[16:24, :] = nsum[8:16, :] + nrecv[1]
         norm_z = [
@@ -819,21 +892,21 @@
         nout[...] = nsum[0:8, :]
 
     def igrad_here(r):
-        return pltpu.make_async_copy(gtwo.at[r], igrad.at[p.own(r), :], out_l.at[1, r])
+        return pltpu.make_async_copy(stage.at[r], igrad.at[p.own(r), :], out_l.at[1, r])
 
     def igrad_pair(rows, r):
-        return remote(gtwo.at[r], igrad.at[rows, :], out_s.at[1, r], out_r.at[1, r], p.pair)
+        return remote(stage.at[r], igrad.at[rows, :], out_s.at[1, r], out_r.at[1, r], p.pair)
 
     def stage_e(r, carry):
+        mixed_here(r).wait()
+        mixed_pair(p.own(r), r).wait_send()
+        mixed_pair(p.other(r), r).wait_recv()
         sum_d.wait(r)
-        gtwo[r] = gtwo[r] + sum_d.total(r, slice(None))
+        stage[r] = (gtwo[r] + sum_d.total(r, slice(None))).astype(BF16)
         igrad_here(r).start()
         igrad_pair(p.own(r), r).start()
         sum_d.close(r)
         pass_on(low_one, 2, p.own(r), r).wait_send()
-        mixed_here(r).wait()
-        mixed_pair(p.own(r), r).wait_send()
-        mixed_pair(p.other(r), r).wait_recv()
         return carry
 
     lax.fori_loop(0, chunks, stage_e, 0)
@@ -842,8 +915,9 @@
             gather.drain()
         scatter_down.finish(outf)
         scatter_up.finish(outf)
-        scatter_a.finish(outa)
-        for scatter in (scatter_down, scatter_up, scatter_a):
+        for scatter in scatter_heads:
+            scatter.finish(outa)
+        for scatter in [scatter_down, scatter_up] + scatter_heads:
             scatter.sent()
         summed = nsum[16:24, :]
         for k in range(1, ring):
@@ -893,11 +967,6 @@
 def interleave(first, second):
     pairs = zip(heads_of(first), heads_of(second))
     return jnp.concatenate([part for pair in pairs for part in pair], axis=1)
-
-
-def split_pair(both):
-    parts = heads_of(both)
-    return jnp.concatenate(parts[::2], axis=1), jnp.concatenate(parts[1::2], axis=1)
 
 
 def pack_attention(attn_in, attn_out):
@@ -915,13 +984,14 @@
 def finish_kernel(*refs):
     grads, (mixed_in, igrad_in), olds = refs[:3], refs[3:5], refs[5:20]
     (mixed, igrad), news, held, made = refs[20:22], refs[22:37], refs[37:55], refs[55:70]
-    passing, (in_sems, out_sems, fetch_sems, copy_sems) = refs[70:72], refs[72:]
+    passing, leaving = refs[70:72], (refs[70], refs[72])
+    in_sems, out_sems, fetch_sems, copy_sems = refs[73:]
     reads = [
         pltpu.make_async_copy(src, dst, in_sems.at[i])
         for i, (src, dst) in enumerate(zip(grads + olds, held))
     ]
     fetches, copies = [], []
-    for src, mid, dst in zip((mixed_in, igrad_in), passing, (mixed, igrad)):
+    for src, mid, end, dst in zip((mixed_in, igrad_in), passing, leaving, (mixed, igrad)):
         size = src.shape[0] // 4
         for part in range(4):
             rows, i = pl.ds(part * size, size), len(copies)
@@ -929,7 +999,7 @@
                 pltpu.make_async_copy(src.at[rows, :], mid.at[rows, :], fetch_sems.at[i])
             )
             copies.append(
-                pltpu.make_async_copy(mid.at[rows, :], dst.at[rows, :], copy_sems.at[i])
+                pltpu.make_async_copy(end.at[rows, :], dst.at[rows, :], copy_sems.at[i])
             )
     for copy in reads + fetches:
         copy.start()
@@ -937,8 +1007,12 @@
         pltpu.make_async_copy(src, dst, out_sems.at[i])
         for i, (src, dst) in enumerate(zip(made, news))
     ]
-    for fetch, copy in zip(fetches, copies):
+    size = igrad.shape[0] // 4
+    for number, (fetch, copy) in enumerate(zip(fetches, copies)):
         fetch.wait()
+        if number >= 4:
+            rows = pl.ds((number - 4) * size, size)
+            leaving[1][rows, :] = passing[1][rows, :].astype(F32)
         copy.start()
     for copy in reads[:3]:
         copy.wait()
@@ -956,9 +1030,10 @@
         for copy in writes[3 * number : 3 * number + 3]:
             copy.start()
 
-    grad_q, grad_k = split_pair(reda[:, :QK])
-    grad_o, grad_v = split_pair(reda[:, QK : 2 * QK])
-    grad_kb, grad_qb = split_pair(reda[:, 2 * QK :])
+    parts = heads_of(reda[...])
+    grad_q, grad_k, grad_o, grad_v, grad_kb, grad_qb = (
+        jnp.concatenate(parts[i::6], axis=1) for i in range(6)
+    )
     update(0, enumerate((grad_q, grad_k, grad_v, grad_qb, grad_kb)), rate_matrix, decay_matrix)
     update(1, [(Ellipsis, grad_o.T)], rate_matrix, decay_matrix)
     update(2, [(Ellipsis, redf[:, :D])], rate_matrix, decay_matrix)
@@ -1030,7 +1105,7 @@
         partial(layer_kernel, ring, chunks),
         out_shape=(
             jax.ShapeDtypeStruct((tokens, D), BF16),
-            jax.ShapeDtypeStruct((tokens, D), F32),
+            jax.ShapeDtypeStruct((tokens, D), BF16),
             jax.ShapeDtypeStruct((share if ring else D, ATT), F32),
             jax.ShapeDtypeStruct((share if ring else D, FFN), F32),
             jax.ShapeDtypeStruct((8, max(share, 128)) if ring else (8, D), F32),
@@ -1047,6 +1122,7 @@
             tile,
             pltpu.VMEM((D, D), BF16),
             pltpu.VMEM((D, QK), BF16),
+            pltpu.VMEM((D // 256, 256, 256), BF16),
             wide,
             wide,
             wide,
@@ -1062,7 +1138,7 @@
             tile,
             tile,
             tile,
-            own_low,
+            pltpu.VMEM((max(chunks, D // 256), HALF, D), BF16),
             pltpu.VMEM((D, FFN), F32),
             pltpu.VMEM((32, D), F32),
             pltpu.VMEM((count + 1, 8, D), F32),
@@ -1088,7 +1164,9 @@
         + [dma(chunks)]
         + [dma(count + 1)] * 2
         + [pltpu.SemaphoreType.DMA]
-        + [dma(3, count)] * 4,
+        + [dma(3, chunks)] * 2
+        + [dma(3)] * 2
+        + [dma(5, count)] * 4,
         compiler_params=pltpu.CompilerParams(
             collective_id=0, has_side_effects=True, vmem_limit_bytes=VMEM_LIMIT
         ),
@@ -1107,14 +1185,17 @@
         + (norm_weight, norm_moment, norm_second)
     )
     large = (mixed, input_grad)
+    wide_grad = jax.ShapeDtypeStruct(input_grad.shape, F32)
     summed = (reda, redf, nred)
     new = pl.pallas_call(
         finish_kernel,
-        out_shape=tuple(jax.ShapeDtypeStruct(part.shape, part.dtype) for part in large + old),
+        out_shape=tuple(
+            jax.ShapeDtypeStruct(part.shape, part.dtype) for part in (mixed, wide_grad) + old
+        ),
         in_specs=[any_space] * 20,
         out_specs=(any_space,) * 17,
         scratch_shapes=[pltpu.VMEM(part.shape, F32) for part in summed + old + old]
-        + [pltpu.VMEM(part.shape, part.dtype) for part in large]
+        + [pltpu.VMEM(part.shape, part.dtype) for part in large + (wide_grad,)]
         + [dma(18), dma(15), dma(8), dma(8)],
         compiler_params=pltpu.CompilerParams(vmem_limit_bytes=VMEM_LIMIT),
     )(*summed, *large, *old)

time: 172 us -> 167 us (0.971)
  Pallas kernels: 171 us -> 166 us
    pallas_call x1, Pallas kernels: 163 us -> 158 us  [per_device(): pl.pallas_call(partial(layer_kernel, ring, chunks), out_shape=(jax.ShapeD...]
where the time goes in v5:
time: 167 us; the launch traced here: 166 us
  Pallas kernels  166 us (99%)
    pallas_call x1, Pallas kernels, per_device(): pl.pallas_call(partial(layer_kernel, ring, chunks), out_shape=(jax.ShapeD...  158 us
    pallas_call x1, Pallas kernels, per_device(): pl.pallas_call(finish_kernel, out_shape=tuple((jax.ShapeDtypeStruct(part....  7.61 us

profile of v5, /device:TPU:0, one launch (start us, length us, event | category | flops | bytes accessed | tf_op | source)
XLA Modules:
  0.0 166.4 jit_solution(2770539567266034372)
XLA Ops:
  0.7 158.0 %shard_map.332 = (bf16[1536,768]{1,0:T(8,128)(2,1)}, bf16[1536,768]{1,0:T(8,128)(2,1)}, f32[96,1152]{1,0:T(8,128)}, f32[96,1536]{1,0:T(8,128)}, f32[8,128]{1,0:T(8,128)}) custom-call(bf16[1536,768]{1,0:T(8,128)(2,1)} %hidden_hbm.1, s32[2,1536]{1,0:T(2,128)} %bitcast.13, s32[12,128]{1,0:T(8,128)} %bitcast.14, s32[12,128]{1,0:T(8,128)} %bitcast.15, ...), custom_call_target="tpu_custom_call" | custom-call | tf_op jit(solution)/shard_map/pallas_call | solution.py:1104
  158.6 7.6 %shard_map.333 = (bf16[1536,768]{1,0:T(8,128)(2,1)}, f32[1536,768]{1,0:T(8,128)}, f32[5,96,192]{2,1,0:T(8,128)}, f32[5,96,192]{2,1,0:T(8,128)}, f32[5,96,192]{2,...) custom-call(f32[96,1152]{1,0:T(8,128)} %get-tuple-element.39.refs_0_, ...), custom_call_target="tpu_custom_call" | custom-call | tf_op jit(solution)/shard_map/pallas_call | solution.py:1190

commit v6 on v5

--- a/solution.py
+++ b/solution.py
@@ -314,6 +314,16 @@
     def middle(self, k):
         self.zsend[k - 1, :, self.cols] = self.added(k).astype(BF16)
         self.zcopy(k).start()
+
+    def kth(self, i):
+        p = self.p
+        place = (p.z // 2 + 1 + i // 2) % (p.ring // 2)
+        line = (i + 1 + p.z) % 2
+        return (2 * place + line + p.ring - p.z) % p.ring
+
+    def middles(self, first, last):
+        for i in range(first, last):
+            self.middle(self.kth(i))
 
     def own(self, out):
         out[:, self.cols] = self.added(0)
@@ -708,9 +718,8 @@
             place = (p.z // 2 + 1 + i) % (ring // 2) if ring else i
             work(pl.ds(pl.multiple_of(place * block, block), block))
             if ring:
-                far = 1 - p.z % 2
-                for line in (far, 1 - far):
-                    scatter.start((2 * place + line + ring - p.z) % ring)
+                for line in range(2):
+                    scatter.start(scatter.kth(2 * i + line))
             return carry
 
         lax.fori_loop(0, D // block, run, 0)
@@ -843,15 +852,17 @@
         context_back(r, 1 - p.half)
         if ring:
 
-            @pl.when(r == min(1, chunks - 1))
+            @pl.when(r == 0)
             def _():
-                for k in range(1, ring):
-                    scatter_down.middle(k)
+                scatter_down.middles(0, ring - 1)
+
+            @pl.when((r == 1) & (r < chunks - 1))
+            def _():
+                scatter_up.middles(0, 1)
 
             @pl.when(r == chunks - 1)
             def _():
-                for k in range(1, ring):
-                    scatter_up.middle(k)
+                scatter_up.middles(1 if chunks > 2 else 0, ring - 1)
                 scatter_down.own(outf)
                 scatter_up.own(outf)
 
@@ -868,15 +879,13 @@
     if ring:
         norm_pair = remote(nsum.at[0:8], nrecv.at[0], ns.at[0], nr.at[0], p.pair)
         norm_pair.start()
-        for k in range(1, ring):
-            scatter_heads[0].middle(k)
+        scatter_heads[0].middles(0, ring - 1)
         norm_pair.wait_recv()
         nsum[8:16, :] = nsum[0:8, :] + nrecv[0]
         norm_x = remote(nsum.at[8:16], nrecv.at[1], ns.at[1], nr.at[1], p.xdev)
         norm_x.start()
         for scatter in scatter_heads[1:]:
-            for k in range(1, ring):
-                scatter.middle(k)
+            scatter.middles(0, ring - 1)
         for scatter in scatter_heads:
             scatter.own(outa)
         norm_x.wait_recv()

time: 167 us -> 166 us (level)
  no operation moved by 1% of the time
where the time goes in v6:
time: 166 us; the launch traced here: 165 us
  Pallas kernels  165 us (99%)
    pallas_call x1, Pallas kernels, per_device(): pl.pallas_call(partial(layer_kernel, ring, chunks), out_shape=(jax.ShapeD...  157 us
    pallas_call x1, Pallas kernels, per_device(): pl.pallas_call(finish_kernel, out_shape=tuple((jax.ShapeDtypeStruct(part....  7.61 us

profile of v6, /device:TPU:0, one launch (start us, length us, event | category | flops | bytes accessed | tf_op | source)
XLA Modules:
  0.0 165.4 jit_solution(13050106873065921454)
XLA Ops:
  0.7 157.0 %shard_map.332 = (bf16[1536,768]{1,0:T(8,128)(2,1)}, bf16[1536,768]{1,0:T(8,128)(2,1)}, f32[96,1152]{1,0:T(8,128)}, f32[96,1536]{1,0:T(8,128)}, f32[8,128]{1,0:T(8,128)}) custom-call(bf16[1536,768]{1,0:T(8,128)(2,1)} %hidden_hbm.1, s32[2,1536]{1,0:T(2,128)} %bitcast.13, s32[12,128]{1,0:T(8,128)} %bitcast.14, s32[12,128]{1,0:T(8,128)} %bitcast.15, ...), custom_call_target="tpu_custom_call" | custom-call | tf_op jit(solution)/shard_map/pallas_call | solution.py:1113
  157.7 7.6 %shard_map.333 = (bf16[1536,768]{1,0:T(8,128)(2,1)}, f32[1536,768]{1,0:T(8,128)}, f32[5,96,192]{2,1,0:T(8,128)}, f32[5,96,192]{2,1,0:T(8,128)}, f32[5,96,192]{2,...) custom-call(f32[96,1152]{1,0:T(8,128)} %get-tuple-element.39.refs_0_, ...), custom_call_target="tpu_custom_call" | custom-call | tf_op jit(solution)/shard_map/pallas_call | solution.py:1199
